TPU v7x, 512 devices: a whole 4x8x8 slice. The times are simulated.
512 devices in a mesh: ch: 512 (over z, y, x, core).
Axes of the slice: x: 4, y: 8, z: 8, core: 2. Of those that a mesh axis runs over, the one named last changes fastest.
Arguments:
- raw: bfloat16 [4096, 65536], P(None, 'ch')
- taps: float32 [16], replicated, may hold values from -1.2 to 1.2
- offsets: int32 [16], replicated, may hold values from 1 to 256, as said below
- sources: int32 [32], replicated, may hold values from 0 to 65535, as said below
- edges: int32 [17], replicated, may hold values from 0 to 128, as said below
Outputs:
- coherence: float32 [16, 32, 65536], P(None, None, 'ch')
- correlation: float32 [32, 129, 65536], P(None, None, 'ch')
Inputs may be any that keep to these rules, and one draw needn't show every extreme that they name: offsets may repeat. `sources`: distinct channels. edges rise; edges[0] = 0, edges[16] = 128, each band holds at least 4 bins.
All inputs are finite; a program needn't handle non-finite values.
Results may differ from a plain program's by a relative error of at most 0.004.
Values may be sent and summed in bfloat16 or wider, within the bound.
No kernel may reach another device: no remote copies, remote signals or barrier semaphores. Data moves between devices by JAX's collectives and lax.ppermute only.
A program may use at most 128 MiB of HBM per device.

v0:
```python
import math

import jax
import jax.numpy as jnp
from jax import lax
from jax.sharding import PartitionSpec as P

SAMPLES = 4096
DEC = 2
TAPS = 16
NFFT = 256
MAXLAG = 64
DECIM = 2048
FRAMES = 8
NBIN = 128
LAGS = 129


def from_behind(block, axis, distance):
    devices = range(lax.axis_size(axis))
    route = [((i - distance) % len(devices), i) for i in devices]
    return lax.ppermute(block, axis, route)


def decimate(samples, taps):
    padded = jnp.pad(samples.astype(jnp.float32), ((TAPS - 1, 0), (0, 0)))
    total = jnp.zeros((DECIM, samples.shape[1]), jnp.float32)
    for j in range(TAPS):
        start = TAPS - 1 - j
        total = total + taps[j] * padded[start : start + SAMPLES : DEC]
    return total


def dft_table():
    index = jnp.arange(NFFT, dtype=jnp.int32)
    bins = jnp.arange(NBIN, dtype=jnp.int32)
    phase = (bins[:, None] * index[None, :] % NFFT).astype(jnp.float32) * (2.0 * math.pi / NFFT)
    return jnp.concatenate([jnp.cos(phase), -jnp.sin(phase)], axis=0)


def lag_table():
    lagvals = jnp.arange(LAGS, dtype=jnp.int32) - MAXLAG
    bins = jnp.arange(NBIN, dtype=jnp.int32)
    phase = (lagvals[:, None] * bins[None, :] % NFFT).astype(jnp.float32) * (2.0 * math.pi / NFFT)
    return jnp.concatenate([jnp.cos(phase), -jnp.sin(phase)], axis=1)


def band_mask(edges):
    bins = jnp.arange(NBIN, dtype=jnp.int32)
    return ((bins[None, :] >= edges[:-1, None]) & (bins[None, :] < edges[1:, None])).astype(
        jnp.float32
    )


def whiten(samples, taps, edges):
    decimated = decimate(samples, taps)
    frames = decimated.reshape(FRAMES, NFFT, samples.shape[1])
    spectrum = jnp.einsum("kn,fnc->fkc", dft_table(), frames, precision=lax.Precision.HIGHEST)
    squares = jnp.sum(spectrum[:, :NBIN] ** 2 + spectrum[:, NBIN:] ** 2, axis=0)
    mask = band_mask(edges)
    counts = jnp.sum(mask, axis=1)
    power = (
        jnp.dot(mask, squares, precision=lax.Precision.HIGHEST) / (2.0 * FRAMES * counts)[:, None]
    )
    level = jnp.sqrt(power + 1e-06)
    per_bin = jnp.dot(mask.T, level, precision=lax.Precision.HIGHEST)
    per_bin = jnp.concatenate([per_bin, per_bin], axis=0)
    return (spectrum / per_bin[None]).astype(jnp.bfloat16)


def band_cross(white, partner, mask, band_scale):
    w_re = white[:, :NBIN].astype(jnp.float32)
    w_im = white[:, NBIN:].astype(jnp.float32)
    p_re = partner[:, :NBIN].astype(jnp.float32)
    p_im = partner[:, NBIN:].astype(jnp.float32)
    cross_re = jnp.sum(w_re * p_re + w_im * p_im, axis=0)
    cross_im = jnp.sum(w_im * p_re - w_re * p_im, axis=0)
    band_re = jnp.dot(mask, cross_re, precision=lax.Precision.HIGHEST) * band_scale[:, None]
    band_im = jnp.dot(mask, cross_im, precision=lax.Precision.HIGHEST) * band_scale[:, None]
    return jnp.concatenate([band_re, band_im], axis=0)


def correlate(source_white, white):
    s_re = source_white[:, :NBIN]
    s_im = source_white[:, NBIN:]
    right = jnp.concatenate([white[:, :NBIN], white[:, NBIN:]], axis=0)
    left_re = jnp.concatenate([s_re, s_im], axis=0)
    left_im = jnp.concatenate([s_im, -s_re], axis=0)
    cross_re = jnp.einsum("fks,fkc->ksc", left_re, right, preferred_element_type=jnp.float32)
    cross_im = jnp.einsum("fks,fkc->ksc", left_im, right, preferred_element_type=jnp.float32)
    cross = jnp.concatenate([cross_re, cross_im], axis=0)
    lagged = jnp.einsum("lk,ksc->slc", lag_table(), cross, precision=lax.Precision.HIGHEST)
    return lagged * (1.0 / math.sqrt(FRAMES * NBIN))


def per_device(raw, taps, offsets, sources, edges):
    width = raw.shape[1]
    white = whiten(raw, taps, edges)
    near_white = from_behind(white, "ch", -1)
    far_white = from_behind(white, "ch", -2)
    extended = jnp.concatenate([white, near_white, far_white], axis=2)
    mask = band_mask(edges)
    band_scale = 1.0 / jnp.sqrt(FRAMES * jnp.sum(mask, axis=1))

    def one_pair(offset):
        partner = lax.dynamic_slice_in_dim(extended, offset, width, 2)
        return band_cross(white, partner, mask, band_scale)

    coherence = lax.map(one_pair, offsets)
    owned = lax.axis_index("ch") * width + jnp.arange(width, dtype=jnp.int32)
    onehot = (owned[:, None] == sources[None, :]).astype(jnp.bfloat16)
    picked = jnp.einsum("fkc,cs->fks", white, onehot, preferred_element_type=jnp.float32)
    source_white = lax.psum(picked, "ch").astype(jnp.bfloat16)
    correlation = correlate(source_white, white)
    return (coherence, correlation)


def solution(mesh):
    in_specs = (P(None, "ch"), P(), P(), P(), P())
    out_specs = (P(None, None, "ch"), P(None, None, "ch"))
    return jax.shard_map(
        per_device, mesh=mesh, in_specs=in_specs, out_specs=out_specs, check_vma=False
    )
```

profile of v0, /device:TPU:1, one launch (start us, length us, event | category | flops | bytes accessed | tf_op | source)
XLA Modules:
  0.0 270.5 jit_solution(9508620658457811836)
XLA Ops:
  0.6 1.4 pad_convert_fusion
  2.1 1.0 slice.135
  3.0 3.5 %slice.137 = f32[2048,128]{1,0:T(8,128)} slice(f32[4111,128]{1,0:T(8,128)S(1)} %pad_convert_fusion), slice={[14:4110:2], [0:128:1]} | slice | bytes 2097152 | tf_op jit(solution)/shard_map/slice | solution.py:30
  6.5 3.5 %slice.139 = f32[2048,128]{1,0:T(8,128)} slice(f32[4111,128]{1,0:T(8,128)S(1)} %pad_convert_fusion), slice={[13:4109:2], [0:128:1]} | slice | bytes 2097152 | tf_op jit(solution)/shard_map/slice | solution.py:30
  10.0 3.4 %slice.141 = f32[2048,128]{1,0:T(8,128)} slice(f32[4111,128]{1,0:T(8,128)S(1)} %pad_convert_fusion), slice={[12:4108:2], [0:128:1]} | slice | bytes 2097152 | tf_op jit(solution)/shard_map/slice | solution.py:30
  13.4 3.5 %slice.143 = f32[2048,128]{1,0:T(8,128)} slice(f32[4111,128]{1,0:T(8,128)S(1)} %pad_convert_fusion), slice={[11:4107:2], [0:128:1]} | slice | bytes 2097152 | tf_op jit(solution)/shard_map/slice | solution.py:30
  16.9 3.5 %slice.145 = f32[2048,128]{1,0:T(8,128)} slice(f32[4111,128]{1,0:T(8,128)S(1)} %pad_convert_fusion), slice={[10:4106:2], [0:128:1]} | slice | bytes 2097152 | tf_op jit(solution)/shard_map/slice | solution.py:30
  20.4 3.5 %slice.147 = f32[2048,128]{1,0:T(8,128)} slice(f32[4111,128]{1,0:T(8,128)S(1)} %pad_convert_fusion), slice={[9:4105:2], [0:128:1]} | slice | bytes 2097152 | tf_op jit(solution)/shard_map/slice | solution.py:30
  23.8 3.5 %slice.149 = f32[2048,128]{1,0:T(8,128)} slice(f32[4111,128]{1,0:T(8,128)S(1)} %pad_convert_fusion), slice={[8:4104:2], [0:128:1]} | slice | bytes 2097152 | tf_op jit(solution)/shard_map/slice | solution.py:30
  27.3 3.5 %slice.151 = f32[2048,128]{1,0:T(8,128)} slice(f32[4111,128]{1,0:T(8,128)S(1)} %pad_convert_fusion), slice={[7:4103:2], [0:128:1]} | slice | bytes 2097152 | tf_op jit(solution)/shard_map/slice | solution.py:30
  30.7 3.5 %slice.153 = f32[2048,128]{1,0:T(8,128)} slice(f32[4111,128]{1,0:T(8,128)S(1)} %pad_convert_fusion), slice={[6:4102:2], [0:128:1]} | slice | bytes 2097152 | tf_op jit(solution)/shard_map/slice | solution.py:30
  34.2 3.5 %slice.155 = f32[2048,128]{1,0:T(8,128)} slice(f32[4111,128]{1,0:T(8,128)S(1)} %pad_convert_fusion), slice={[5:4101:2], [0:128:1]} | slice | bytes 2097152 | tf_op jit(solution)/shard_map/slice | solution.py:30
  37.7 3.5 %slice.157 = f32[2048,128]{1,0:T(8,128)} slice(f32[4111,128]{1,0:T(8,128)S(1)} %pad_convert_fusion), slice={[4:4100:2], [0:128:1]} | slice | bytes 2097152 | tf_op jit(solution)/shard_map/slice | solution.py:30
  41.2 3.5 %slice.159 = f32[2048,128]{1,0:T(8,128)} slice(f32[4111,128]{1,0:T(8,128)S(1)} %pad_convert_fusion), slice={[3:4099:2], [0:128:1]} | slice | bytes 2097152 | tf_op jit(solution)/shard_map/slice | solution.py:30
  44.6 3.5 %slice.161 = f32[2048,128]{1,0:T(8,128)} slice(f32[4111,128]{1,0:T(8,128)S(1)} %pad_convert_fusion), slice={[2:4098:2], [0:128:1]} | slice | bytes 2097152 | tf_op jit(solution)/shard_map/slice | solution.py:30
  48.1 3.5 %slice.163 = f32[2048,128]{1,0:T(8,128)} slice(f32[4111,128]{1,0:T(8,128)S(1)} %pad_convert_fusion), slice={[1:4097:2], [0:128:1]} | slice | bytes 2097152 | tf_op jit(solution)/shard_map/slice | solution.py:30
  51.6 3.5 %slice.165 = f32[2048,128]{1,0:T(8,128)} slice(f32[4111,128]{1,0:T(8,128)S(1)} %pad_convert_fusion), slice={[0:4096:2], [0:128:1]} | slice | bytes 2097152 | tf_op jit(solution)/shard_map/slice | solution.py:30
  55.0 0.5 sine_negate_fusion
  55.6 0.7 fusion.62
  56.3 16.9 %multiply_add_fusion = f32[2048,128]{1,0:T(8,128)S(1)} fusion(f32[2048,128]{1,0:T(8,128)} %slice.165, f32[2048,128]{1,0:T(8,128)} %slice.163, f32[2048,128]{1,0:T(8,128)} %slice.161, f32[2048,128]{1,0:T(8,128)} %slice.159, f32[2048,128]{1,0:T(8,128)} %slice.157, f32[2048,128]{1,0:T(8,128)} %slice.155, f32[2048,128]{1,0:T(8,128)} %slice.153, ...), kind=kLoop, calls=%fused_computation.37 | loop fusion | flops 8126464 | bytes 17825856 | tf_op jit(solution)/shard_map/add | solution.py:30
  73.2 1.8 convolution_bitcast_fusion
  75.6 0.3 fusion.50
  76.2 8.8 %collective-permute-start = (bf16[8,256,128]{1,2,0:T(8,128)(2,1)S(1)}, bf16[8,256,128]{1,2,0:T(8,128)(2,1)S(1)}, u32[]{:S(2)}, u32[]{:S(2)}) collective-permute-start(bf16[8,256,128]{1,2,0:T(8,128)(2,1)S(1)} %divide_convert_fusion), channel_id=1, source_target_pairs={{1,0},{2,1},{3,2},{4,3},{5,4},{6,5},{7,6},{8,7},{9,8},{10,9},{11,1... | collective-permute-start | bytes 1572872 | tf_op jit(solution)/shard_map/ppermute | solution.py:22
  85.0 10.4 %collective-permute-start.1 = (bf16[8,256,128]{1,2,0:T(8,128)(2,1)S(1)}, bf16[8,256,128]{1,2,0:T(8,128)(2,1)}, u32[]{:S(2)}, u32[]{:S(2)}) collective-permute-start(bf16[8,256,128]{1,2,0:T(8,128)(2,1)S(1)} %divide_convert_fusion), channel_id=1, source_target_pairs={{2,0},{3,1},{4,2},{5,3},{6,4},{7,5},{8,6},{9,7},{10,8},{11,9},{12,... | collective-permute-start | bytes 1572872 | tf_op jit(solution)/shard_map/ppermute | solution.py:22
  95.5 0.3 copy.21
  95.9 0.4 copy.25
  96.3 0.2 fusion.44
  96.6 103.3 %all-reduce.2 = bf16[8,256,32]{1,2,0:T(8,128)(2,1)S(1)} all-reduce(f32[8,256,32]{1,2,0:T(8,128)S(1)} %fusion.44), channel_id=1, replica_groups=mesh['ch'=512] {'ch'}, use_global_device_ids=true, to_apply=%region_6.7 | all-reduce | flops 65536 | bytes 393216 | tf_op jit(solution)/shard_map/psum | solution.py:113
  199.9 0.4 copy.24
  200.4 0.4 copy.26
  200.8 0.5 fusion.63
  201.3 0.5 fusion.64
  201.9 0.4 fusion.43
  202.2 0.4 pad_maximum_fusion
  202.7 5.0 %multiply_bitcast_fusion = f32[32,129,128]{2,1,0:T(8,128)S(1)} fusion(f32[256,32,128]{2,1,0:T(8,128)S(1)} %pad_maximum_fusion, f32[129,128]{1,0:T(8,128)S(1)} %get-tuple-element.118, f32[129,128]{1,0:T(8,128)S(1)} %get-tuple-element.117), kind=kOutput, calls=%fused_computation.29 | convolution fusion | flops 1623757056 | bytes 6439936 | tf_op jit(solution)/shard_map/lk,ksc->slc/dot_general | solution.py:92
  207.6 1.7 copy.29
  209.4 1.1 pad_maximum_fusion.1
  210.5 59.3 %while.11 = (s32[]{:T(128)}, f32[16,32,128]{2,1,0:T(8,128)S(1)}, bf16[8,256,128]{2,1,0:T(8,128)(2,1)S(1)}, s32[16]{0:T(128)S(1)}, bf16[8,256,384]{1,2,0:T(8,128)...) while((s32[]{:T(128)}, f32[16,32,128]{2,1,0:T(8,128)S(1)}, ...), condition=%wide.region_5.6_spmd.clone, body=%wide.region_2.5_spmd.clone.sunk | while | flops 7856134 | bytes 3457595 | solution.py:109
  210.5 0.6 dynamic_slice.10
  214.2 0.6 dynamic_slice.10
  217.7 0.2 fusion.89
  218.0 0.6 dynamic_slice.10
  221.4 0.2 fusion.89
  221.7 0.6 dynamic_slice.10
  225.1 0.2 fusion.89
  225.4 0.6 dynamic_slice.10
  228.8 0.2 fusion.89
  229.1 0.6 dynamic_slice.10
  232.5 0.2 fusion.89
  232.8 0.6 dynamic_slice.10
  236.2 0.2 fusion.89
  236.5 0.6 dynamic_slice.10
  239.9 0.2 fusion.89
  240.2 0.6 dynamic_slice.10
  243.6 0.2 fusion.89
  243.9 0.6 dynamic_slice.10
  247.6 0.6 dynamic_slice.10
  251.0 0.2 fusion.89
  251.3 0.6 dynamic_slice.10
  255.0 0.6 dynamic_slice.10
  258.7 0.6 dynamic_slice.10
  262.4 0.6 dynamic_slice.10
  266.1 0.6 dynamic_slice.10
  269.8 0.7 copy-done.3
  (129 shorter events, 18.4 us)
Async XLA Ops:
  48.1 7.5 %copy-start = (f32[16]{0:T(128)S(1)}, f32[16]{0:T(128)}, u32[]{:S(2)}) copy-start(f32[16]{0:T(128)} %param.8) | copy-start | bytes 196
  73.2 2.0 copy-start.1
  76.2 20.2 %copy-start.2 = (s32[32]{0:T(128)S(1)}, s32[32]{0:T(128)}, u32[]{:S(2)}) copy-start(s32[32]{0:T(128)} %param.10) | copy-start | bytes 388
  76.2 133.2 %collective-permute-start = (bf16[8,256,128]{1,2,0:T(8,128)(2,1)S(1)}, bf16[8,256,128]{1,2,0:T(8,128)(2,1)S(1)}, u32[]{:S(2)}, u32[]{:S(2)}) collective-permute-start(bf16[8,256,128]{1,2,0:T(8,128)(2,1)S(1)} %divide_convert_fusion), channel_id=1, source_target_pairs={{1,0},{2,1},{3,2},{4,3},{5,4},{6,5},{7,6},{8,7},{9,8},{10,9},{11,1... | collective-permute-start | bytes 1572872 | tf_op jit(solution)/shard_map/ppermute | solution.py:22
  85.0 124.4 %collective-permute-start.1 = (bf16[8,256,128]{1,2,0:T(8,128)(2,1)S(1)}, bf16[8,256,128]{1,2,0:T(8,128)(2,1)}, u32[]{:S(2)}, u32[]{:S(2)}) collective-permute-start(bf16[8,256,128]{1,2,0:T(8,128)(2,1)S(1)} %divide_convert_fusion), channel_id=1, source_target_pairs={{2,0},{3,1},{4,2},{5,3},{6,4},{7,5},{8,6},{9,7},{10,8},{11,9},{12,... | collective-permute-start | bytes 1572872 | tf_op jit(solution)/shard_map/ppermute | solution.py:22
  209.4 1.2 copy-start.4
  269.8 0.7 copy-start.3
where the time goes:
time: 273 us; the launch traced here: 271 us
  blocking collectives  103 us (38%)
  local copies, waits for them, and re-layouts  76.6 us (28%)
  loops' own time  30 us (11%)
  other arithmetic  25.1 us (9%)
  starting transfers between devices  19.2 us (7%)
  matrix products  15.4 us (6%)
    psum x1, blocking collectives, per_device(): source_white = lax.psum(picked, 'ch').astype(jnp.bfloat16)  103 us
    slice x17, local copies, waits for them, and re-layouts, decimate(): total = total + taps[j] * padded[start:start + SAMPLES:DEC]  53.7 us
    another operation x1, loops' own time, per_device(): coherence = lax.map(one_pair, offsets)  30 us
    ppermute x2, starting transfers between devices, from_behind(): return lax.ppermute(block, axis, route)  19.2 us
    add x1, other arithmetic, decimate(): total = total + taps[j] * padded[start:start + SAMPLES:DEC]  16.9 us
    dynamic_slice x16, local copies, waits for them, and re-layouts, per_device(): coherence = lax.map(one_pair, offsets)  9.87 us
    while x32, local copies, waits for them, and re-layouts  5.75 us
  transfers between devices with their start and end apart: 2, of which 0 were waited for; matrix products, arithmetic and copies ran while one was open for 4% of the time, Pallas kernels for 0%

commit v1 on v0

v1 whole, which is shorter than its diff:
```python
import math

import jax
import jax.numpy as jnp
import numpy as np
from jax import lax
from jax.experimental import pallas as pl
from jax.experimental.pallas import tpu as pltpu
from jax.sharding import PartitionSpec as P

SAMPLES = 4096
TAPS = 16
NFFT = 256
FRAMES = 8
NBIN = 128
BANDS = 16
SOURCES = 32
OFFS = 16
MAXLAG = 64
LAGS = 129
LAG_ROWS = 144
WIDTH = 128
HALO = 16
SPAN = 2 * NFFT + HALO
CHUNK = 16
CHUNKS = NBIN // CHUNK
VMEM_LIMIT = 48 * 1024 * 1024
F32 = jnp.float32
BF16 = jnp.bfloat16


def dft_table():
    phase = np.arange(NBIN)[:, None] * np.arange(NFFT)[None, :] % NFFT * (2.0 * math.pi / NFFT)
    return np.concatenate([np.cos(phase), -np.sin(phase)], axis=0).astype(np.float32)


def lag_tables():
    lags = np.arange(LAGS) - MAXLAG
    phase = lags[:, None] * np.arange(NBIN)[None, :] % NFFT * (2.0 * math.pi / NFFT)
    table = np.concatenate([np.cos(phase), -np.sin(phase)], axis=1) / math.sqrt(FRAMES * NBIN)
    table = np.pad(table, ((0, LAG_ROWS - LAGS), (0, 0))).astype(np.float32)
    high = table.astype(BF16)
    low = (table - high.astype(np.float32)).astype(BF16)
    return np.concatenate([high, low], axis=0)


def split(x, parts):
    out = []
    for _ in range(parts):
        piece = lax.reduce_precision(x, 8, 7)
        out.append(piece.astype(BF16))
        x = x - piece
    return out


def filtered_table(taps):
    n = lax.broadcasted_iota(jnp.int32, (NFFT, SPAN), 0)
    i = lax.broadcasted_iota(jnp.int32, (NFFT, SPAN), 1)
    which = 2 * n + HALO - i
    spread = jnp.zeros((NFFT, SPAN), F32)
    for j in range(TAPS):
        spread = jnp.where(which == j, taps[j], spread)
    table = jnp.dot(jnp.asarray(dft_table()), spread, precision=lax.Precision.HIGHEST)
    return jnp.stack(split(table, 3))


def chunk_rows(white, c):
    rows = []
    for f in range(FRAMES):
        for part in range(2):
            start = part * NBIN + c * CHUNK
            rows.append(white[f, start : start + CHUNK, :])
    return rows


def whiten_kernel(table, raw, mask, counts, onehot, white, picked, spectrum):
    squares = jnp.zeros((NFFT, WIDTH), F32)
    for f in range(FRAMES):
        total = jnp.zeros((NFFT, WIDTH), F32)
        for part in range(3):
            if f == 0:
                total += jnp.dot(
                    table[part, :, HALO:], raw[: 2 * NFFT, :], preferred_element_type=F32
                )
            else:
                start = f * 2 * NFFT - HALO
                total += jnp.dot(
                    table[part], raw[start : start + SPAN, :], preferred_element_type=F32
                )
        spectrum[f] = total
        squares += total * total
    squares = squares[:NBIN] + squares[NBIN:]
    power = jnp.dot(mask[...], squares, precision=lax.Precision.HIGHEST) / counts[...]
    level = jnp.sqrt(power + 1e-06)
    per_bin = lax.dot_general(
        mask[...], level, (((0,), (0,)), ((), ())), precision=lax.Precision.HIGHEST
    )
    inverse = 1.0 / per_bin
    for f in range(FRAMES):
        white[f, :NBIN, :] = (spectrum[f, :NBIN, :] * inverse).astype(BF16)
        white[f, NBIN:, :] = (spectrum[f, NBIN:, :] * inverse).astype(BF16)
    for c in range(CHUNKS):
        rows = jnp.concatenate(chunk_rows(white, c), axis=0)
        found = lax.dot_general(
            onehot[...], rows, (((1,), (1,)), ((), ())), preferred_element_type=F32
        ).astype(BF16)
        picked[2 * c] = found[:, :WIDTH]
        picked[2 * c + 1] = found[:, WIDTH:]


def whiten(raw, taps, mask, onehot):
    counts = 2.0 * FRAMES * jnp.sum(mask, axis=1, keepdims=True)
    return pl.pallas_call(
        whiten_kernel,
        out_shape=(
            jax.ShapeDtypeStruct((FRAMES, NFFT, WIDTH), BF16),
            jax.ShapeDtypeStruct((2 * CHUNKS, SOURCES, WIDTH), BF16),
        ),
        scratch_shapes=[pltpu.VMEM((FRAMES, NFFT, WIDTH), F32)],
        compiler_params=pltpu.CompilerParams(vmem_limit_bytes=VMEM_LIMIT),
        name="whiten",
    )(filtered_table(taps), raw, mask, counts, onehot)


def coherence_kernel(offsets, mask, scale, own, near, far, out, ext, base, high, low):
    for f in range(FRAMES):
        base[f] = own[f].astype(F32)
        ext[0, f] = base[f]
        ext[1, f] = near[f].astype(F32)
        ext[2, f] = far[f].astype(F32)
    lane = lax.broadcasted_iota(jnp.int32, (1, WIDTH), 1)
    step = 32

    def pair(p, _):
        offset = offsets[p]
        first = offset // WIDTH
        second = jnp.minimum(first + 1, 2)
        turn = offset % WIDTH
        wrapped = jnp.broadcast_to(lane < turn, (step, WIDTH))
        shift = (WIDTH - turn) % WIDTH

        def partner(f, start):
            a = ext[first, f, start : start + step, :]
            b = ext[second, f, start : start + step, :]
            return pltpu.roll(jnp.where(wrapped, b, a), shift, 1)

        for k in range(0, NBIN, step):
            real = jnp.zeros((step, WIDTH), F32)
            imag = jnp.zeros((step, WIDTH), F32)
            for f in range(FRAMES):
                p_re, p_im = partner(f, k), partner(f, NBIN + k)
                w_re = base[f, k : k + step, :]
                w_im = base[f, NBIN + k : NBIN + k + step, :]
                real += w_re * p_re + w_im * p_im
                imag += w_im * p_re - w_re * p_im
            for part, cross in enumerate((real, imag)):
                top = cross.astype(BF16)
                high[p, part, k : k + step, :] = top
                low[p, part, k : k + step, :] = (cross - top.astype(F32)).astype(BF16)
        return 0

    lax.fori_loop(0, OFFS, pair, 0)
    bands = mask[...].astype(BF16)
    for p in range(OFFS):
        for part in range(2):
            total = jnp.dot(bands, high[p, part], preferred_element_type=F32)
            total += jnp.dot(bands, low[p, part], preferred_element_type=F32)
            out[p, part * BANDS : (part + 1) * BANDS, :] = total * scale[...]


def coherences(offsets, mask, own, near, far):
    scale = 1.0 / jnp.sqrt(FRAMES * jnp.sum(mask, axis=1, keepdims=True))
    vmem = pl.BlockSpec(memory_space=pltpu.VMEM)
    return pl.pallas_call(
        coherence_kernel,
        out_shape=jax.ShapeDtypeStruct((OFFS, 2 * BANDS, WIDTH), F32),
        in_specs=[pl.BlockSpec(memory_space=pltpu.SMEM)] + [vmem] * 5,
        out_specs=vmem,
        scratch_shapes=[
            pltpu.VMEM((3, FRAMES, NFFT, WIDTH), F32),
            pltpu.VMEM((FRAMES, NFFT, WIDTH), F32),
            pltpu.VMEM((OFFS, 2, NBIN, WIDTH), BF16),
            pltpu.VMEM((OFFS, 2, NBIN, WIDTH), BF16),
        ],
        compiler_params=pltpu.CompilerParams(vmem_limit_bytes=VMEM_LIMIT),
        name="coherence",
    )(offsets, mask, scale, own, near, far)


S_STEP = 4


def correlate_kernel(table, sources, white, out, left, high, low):
    @pl.when(pl.program_id(0) == 0)
    def _():
        row = lax.broadcasted_iota(jnp.int32, (CHUNK, NFFT), 0)
        column = lax.broadcasted_iota(jnp.int32, (CHUNK, NFFT), 1)
        diagonal = (column % CHUNK) == row
        for c in range(CHUNKS):
            values = jnp.concatenate([sources[2 * c], sources[2 * c + 1]], axis=1).astype(F32)
            for s in range(SOURCES):
                spread = jnp.broadcast_to(values[s : s + 1, :], (CHUNK, NFFT))
                left[s * CHUNK : (s + 1) * CHUNK, :] = jnp.where(diagonal, spread, 0.0).astype(BF16)
            rows = chunk_rows(white, c)
            turned = []
            for f in range(FRAMES):
                turned += [-rows[2 * f + 1], rows[2 * f]]
            right = jnp.concatenate(
                [jnp.concatenate(rows, axis=0), jnp.concatenate(turned, axis=0)], axis=1
            )
            cross = jnp.dot(left[...], right, preferred_element_type=F32)
            top = cross.astype(BF16)
            rest = (cross - top.astype(F32)).astype(BF16)
            for kept, value in ((high, top), (low, rest)):
                value = value.reshape(SOURCES, CHUNK, 2 * WIDTH)
                for part in range(2):
                    start = part * NBIN + c * CHUNK
                    kept[:, start : start + CHUNK, :] = value[:, :, part * WIDTH : (part + 1) * WIDTH]

    base = pl.program_id(0) * S_STEP
    for i in range(0, S_STEP, 2):
        top = jnp.concatenate([high[base + i], high[base + i + 1]], axis=1)
        rest = jnp.concatenate([low[base + i], low[base + i + 1]], axis=1)
        both = jnp.dot(table[...], top, preferred_element_type=F32)
        lagged = both[:LAG_ROWS] + both[LAG_ROWS:]
        lagged += jnp.dot(table[:LAG_ROWS, :], rest, preferred_element_type=F32)
        out[i] = lagged[:LAGS, :WIDTH]
        out[i + 1] = lagged[:LAGS, WIDTH:]


def correlations(sources, white):
    return pl.pallas_call(
        correlate_kernel,
        grid=(SOURCES // S_STEP,),
        out_shape=jax.ShapeDtypeStruct((SOURCES, LAGS, WIDTH), F32),
        in_specs=[
            pl.BlockSpec((2 * LAG_ROWS, NFFT), lambda g: (0, 0)),
            pl.BlockSpec((2 * CHUNKS, SOURCES, WIDTH), lambda g: (0, 0, 0)),
            pl.BlockSpec((FRAMES, NFFT, WIDTH), lambda g: (0, 0, 0)),
        ],
        out_specs=pl.BlockSpec((S_STEP, LAGS, WIDTH), lambda g: (g, 0, 0)),
        scratch_shapes=[
            pltpu.VMEM((SOURCES * CHUNK, NFFT), BF16),
            pltpu.VMEM((SOURCES, NFFT, WIDTH), BF16),
            pltpu.VMEM((SOURCES, NFFT, WIDTH), BF16),
        ],
        compiler_params=pltpu.CompilerParams(vmem_limit_bytes=VMEM_LIMIT),
        name="correlate",
    )(jnp.asarray(lag_tables()), sources, white)


def from_behind(block, axis, distance):
    devices = range(lax.axis_size(axis))
    route = [((i - distance) % len(devices), i) for i in devices]
    return lax.ppermute(block, axis, route)


def groups_of(size, inner):
    if inner:
        return [list(range(g * inner, (g + 1) * inner)) for g in range(size // inner)]
    return [list(range(g, size, 16)) for g in range(16)]


def spread_sources(picked):
    size = lax.axis_size("ch")
    runs = groups_of(size, 16)
    places = groups_of(size, 0)
    mine = lax.all_to_all(picked, "ch", 0, 0, axis_index_groups=runs, tiled=True)
    mine = jnp.sum(mine.astype(F32), axis=0).astype(BF16)
    copies = jnp.broadcast_to(mine[None], (len(places[0]),) + mine.shape)
    mine = lax.all_to_all(copies, "ch", 0, 0, axis_index_groups=places, tiled=True)
    mine = jnp.sum(mine.astype(F32), axis=0).astype(BF16)
    copies = jnp.broadcast_to(mine[None], (len(runs[0]),) + mine.shape)
    return lax.all_to_all(copies, "ch", 0, 0, axis_index_groups=runs, tiled=True)


def per_device(raw, taps, offsets, sources, edges):
    bins = jnp.arange(NBIN, dtype=jnp.int32)
    mask = ((bins[None, :] >= edges[:-1, None]) & (bins[None, :] < edges[1:, None])).astype(F32)
    owned = lax.axis_index("ch") * WIDTH + jnp.arange(WIDTH, dtype=jnp.int32)
    onehot = (sources[:, None] == owned[None, :]).astype(BF16)
    white, picked = whiten(raw, taps, mask, onehot)
    near = from_behind(white, "ch", -1)
    far = from_behind(white, "ch", -2)
    coherence = coherences(offsets, mask, white, near, far)
    correlation = correlations(spread_sources(picked), white)
    return (coherence, correlation)


def solution(mesh):
    in_specs = (P(None, "ch"), P(), P(), P(), P())
    out_specs = (P(None, None, "ch"), P(None, None, "ch"))
    return jax.shard_map(
        per_device, mesh=mesh, in_specs=in_specs, out_specs=out_specs, check_vma=False
    )
```

time: 273 us -> 88.8 us (0.33)
  the two profiles are of different devices: /device:TPU:1 before, /device:TPU:31 now
where the time goes in v1:
time: 88.8 us; the launch traced here: 88.2 us
  starting transfers between devices  29.3 us (33%)
  Pallas kernels  13.9 us (16%)
  waiting for transfers between devices  13.7 us (15%)
  matrix products  12.6 us (14%)
  blocking collectives  9.67 us (11%)
  local copies, waits for them, and re-layouts  7.1 us (8%)
  other arithmetic  1.24 us (1%)
    all_to_all x1, starting transfers between devices, spread_sources(): lax.all_to_all(copies, 'ch', 0, 0, axis_index_groups=places, tiled=True)  14.6 us
    dot_general x1, matrix products, filtered_table(): jnp.dot(jnp.asarray(dft_table()), spread, precision=lax.Precision.HIGHEST)  12.6 us
    all_to_all x1, blocking collectives, spread_sources(): lax.all_to_all(picked, 'ch', 0, 0, axis_index_groups=runs, tiled=True)  9.67 us
    all_to_all x1, starting transfers between devices, spread_sources(): lax.all_to_all(copies, 'ch', 0, 0, axis_index_groups=runs, tiled=True)  9.42 us
    ppermute x2, waiting for transfers between devices, from_behind(): return lax.ppermute(block, axis, route)  7.92 us
    pallas_call x1, Pallas kernels, coherences(): pl.pallas_call(coherence_kernel, out_shape=jax.ShapeDtypeStruct((OFFS, 2...  7.84 us
    all_to_all x1, waiting for transfers between devices, spread_sources(): lax.all_to_all(copies, 'ch', 0, 0, axis_index_groups=places, tiled=True)  5.82 us
    ppermute x2, starting transfers between devices, from_behind(): return lax.ppermute(block, axis, route)  5.28 us
  transfers between devices with their start and end apart: 4, of which 3 were waited for; matrix products, arithmetic and copies ran while one was open for 1% of the time, Pallas kernels for 9%

profile of v1, /device:TPU:31, one launch (start us, length us, event | category | flops | bytes accessed | tf_op | source)
XLA Modules:
  0.0 88.2 jit_solution(8197611650067594851)
XLA Ops:
  0.6 0.8 fusion.109
  1.4 0.2 fusion.90
  1.6 0.1 fusion.89.mask
  1.7 0.1 copy.16.counts
  1.8 2.0 %fusion.108 = (f32[1]{0:T(128)}, f32[1]{0:T(128)}, f32[1]{0:T(128)}, f32[1]{0:T(128)}, f32[1]{0:T(128)}, /*index=5*/f32[1]{0:T(128)}, f32[1]{0:T(128)}, f32[1]{0...) fusion(f32[16]{0:T(128)} %param.8), kind=kLoop, calls=%fused_computation.105 | loop fusion | bytes 128 | tf_op jit(solution)/shard_map/slice | solution.py:62
  3.8 0.7 compare_convert_fusion.onehot
  4.5 12.6 %fusion.52 = (bf16[1,256,528]{2,1,0:T(8,128)(2,1)S(1)}, bf16[1,256,528]{2,1,0:T(8,128)(2,1)S(1)}, bf16[1,256,528]{2,1,0:T(8,128)(2,1)S(1)}) fusion(f32[256,256]{1,0:T(8,128)} %constant.55.clone, f32[]{:T(128)} %bitcast.16, f32[]{:T(128)} %bitcast.15, f32[]{:T(128)} %bitcast.14, f32[]{:T(128)} %bitcast.13, f32[]{:T(128)} %bitcast.12, f32[]{:T(128)} %bitcast.11, ...), kind=kOutput, calls=%fused_computation.42 | convolution fusion | flops 420777984 | bytes 1074240 | tf_op jit(solution)/shard_map/dot_general | solution.py:63
  17.1 0.0 copy-start
  17.1 0.2 pad_maximum_fusion.table
  17.3 1.0 %copy-done = bf16[4096,128]{1,0:T(8,128)(2,1)S(1)} copy-done((bf16[4096,128]{1,0:T(8,128)(2,1)S(1)}, bf16[4096,128]{1,0:T(8,128)(2,1)}, u32[]{:S(2)}) %copy-start) | copy-done | bytes 1048600
  18.3 0.0 copy-start.2
  18.3 3.0 %whiten.1 = (bf16[8,256,128]{2,1,0:T(8,128)(2,1)S(1)}, bf16[16,32,128]{2,1,0:T(8,128)(2,1)S(1)}) custom-call(bf16[3,256,528]{2,1,0:T(8,128)(2,1)S(1)} %pad_maximum_fusion.table, bf16[4096,128]{1,0:T(8,128)(2,1)S(1)} %copy-done, f32[16,128]{1,0:T(8,128)S(1)} %fusion.89.mask, f32[16,1]{1,0:T(8,128)S(1)} %copy.16.counts, ...), custom_call_target="tpu_custom_call" | custom-call | tf_op jit(solution)/shard_map/whiten/pallas_call | solution.py:113
  21.3 0.0 copy-start.1
  21.3 9.7 %all_to_all.15 = bf16[16,32,128]{2,1,0:T(8,128)(2,1)S(1)} all-to-all(bf16[16,32,128]{2,1,0:T(8,128)(2,1)S(1)} %get-tuple-element.5), channel_id=1, replica_groups={{0,1,2,3,4,5,6,7,8,9,10,11,12,13,14,15},{16,17,18,19,20,21,22,23,24,25,..., dimensions={0} | all-to-all | bytes 262144 | tf_op jit(solution)/shard_map/all_to_all | solution.py:268
  31.0 0.7 broadcast_in_dim.89
  31.7 14.6 %all-to-all-start.1 = ((bf16[32,32,128]{2,1,0:T(8,128)(2,1)}), bf16[32,32,128]{2,1,0:T(8,128)(2,1)S(1)}, u32[]{:S(2)}, u32[]{:S(2)}) async-start(bf16[32,32,128]{2,1,0:T(8,128)(2,1)} %broadcast_in_dim.89), calls=%async_computation.1 | async-start | bytes 524288 | tf_op jit(solution)/shard_map/all_to_all | solution.py:271
  46.4 2.2 %collective-permute-start.1 = (bf16[8,256,128]{2,1,0:T(8,128)(2,1)S(1)}, bf16[8,256,128]{2,1,0:T(8,128)(2,1)S(1)}, u32[]{:S(2)}, u32[]{:S(2)}) collective-permute-start(bf16[8,256,128]{2,1,0:T(8,128)(2,1)S(1)} %get-tuple-element.4.own.white), channel_id=1, source_target_pairs={{2,0},{3,1},{4,2},{5,3},{6,4},{7,5},{8,6},{9,7},{10,8},{11,9},{12,... | collective-permute-start | bytes 1572872 | tf_op jit(solution)/shard_map/ppermute | solution.py:255
  48.6 3.1 %collective-permute-start = (bf16[8,256,128]{2,1,0:T(8,128)(2,1)S(1)}, bf16[8,256,128]{2,1,0:T(8,128)(2,1)S(1)}, u32[]{:S(2)}, u32[]{:S(2)}) collective-permute-start(bf16[8,256,128]{2,1,0:T(8,128)(2,1)S(1)} %get-tuple-element.4.own.white), channel_id=1, source_target_pairs={{1,0},{2,1},{3,2},{4,3},{5,4},{6,5},{7,6},{8,7},{9,8},{10,9},{11,1... | collective-permute-start | bytes 1572872 | tf_op jit(solution)/shard_map/ppermute | solution.py:255
  51.6 5.8 %all-to-all-done.1 = bf16[32,32,128]{2,1,0:T(8,128)(2,1)S(1)} async-done(((bf16[32,32,128]{2,1,0:T(8,128)(2,1)}), bf16[32,32,128]{2,1,0:T(8,128)(2,1)S(1)}, u32[]{:S(2)}, u32[]{:S(2)}) %all-to-all-start.1) | async-done | bytes 262176 | tf_op jit(solution)/shard_map/all_to_all | solution.py:271
  57.5 0.1 reduce_sum.39
  57.5 0.7 broadcast_in_dim.90
  58.2 9.4 %all-to-all-start.2 = ((bf16[16,32,128]{2,1,0:T(8,128)(2,1)}), bf16[16,32,128]{2,1,0:T(8,128)(2,1)S(1)}, u32[]{:S(2)}, u32[]{:S(2)}) async-start(bf16[16,32,128]{2,1,0:T(8,128)(2,1)} %broadcast_in_dim.90), calls=%async_computation.2 | async-start | bytes 262144 | tf_op jit(solution)/shard_map/all_to_all | solution.py:274
  67.6 0.1 copy.17.scale
  67.7 1.1 %collective-permute-done.1.far = bf16[8,256,128]{2,1,0:T(8,128)(2,1)S(1)} collective-permute-done((bf16[8,256,128]{2,1,0:T(8,128)(2,1)S(1)}, bf16[8,256,128]{2,1,0:T(8,128)(2,1)S(1)}, u32[]{:S(2)}, u32[]{:S(2)}) %collective-permute-start.1) | collective-permute-done | bytes 524320 | tf_op jit(solution)/shard_map/ppermute | solution.py:255
  68.8 6.8 %collective-permute-done.near = bf16[8,256,128]{2,1,0:T(8,128)(2,1)S(1)} collective-permute-done((bf16[8,256,128]{2,1,0:T(8,128)(2,1)S(1)}, bf16[8,256,128]{2,1,0:T(8,128)(2,1)S(1)}, u32[]{:S(2)}, u32[]{:S(2)}) %collective-permute-start) | collective-permute-done | bytes 524320 | tf_op jit(solution)/shard_map/ppermute | solution.py:255
  75.6 0.0 copy-done.2
  75.6 7.8 %coherence.1 = f32[16,32,128]{2,1,0:T(8,128)} custom-call(s32[16]{0:T(128)S(1)} %copy-done.2, f32[16,128]{1,0:T(8,128)S(1)} %fusion.89.mask, f32[16,1]{1,0:T(8,128)S(1)} %copy.17.scale, bf16[8,256,128]{2,1,0:T(8,128)(2,1)S(1)} %get-tuple-element.4.own.white, bf16[8,256,128]{2,1,0:T(8,128)(2,1)S(1)} %collective-permute-done.near, ...), custom_call_target="tpu_custom_call" | custom-call | tf_op jit(solution)/shard_map/coherence/pallas_call | solution.py:174
  83.5 0.0 all-to-all-done.2.sources
  83.5 0.0 copy-done.1
  83.5 3.0 %correlate.1 = f32[32,129,128]{2,1,0:T(8,128)S(1)} custom-call(bf16[288,256]{1,0:T(8,128)(2,1)S(1)} %copy-done.1, bf16[16,32,128]{2,1,0:T(8,128)(2,1)S(1)} %all-to-all-done.2.sources, bf16[8,256,128]{2,1,0:T(8,128)(2,1)S(1)} %get-tuple-element.4.own.white), custom_call_target="tpu_custom_call" | custom-call | tf_op jit(solution)/shard_map/correlate/pallas_call | solution.py:232
  86.5 1.7 %copy.18 = f32[32,129,128]{2,0,1:T(8,128)} copy(f32[32,129,128]{2,1,0:T(8,128)S(1)} %correlate.1) | data formatting | bytes 4227072
  (4 shorter events, 0.0 us)
Async XLA Ops:
  17.1 1.2 %copy-start = (bf16[4096,128]{1,0:T(8,128)(2,1)S(1)}, bf16[4096,128]{1,0:T(8,128)(2,1)}, u32[]{:S(2)}) copy-start(bf16[4096,128]{1,0:T(8,128)(2,1)} %raw.1) | copy-start | bytes 3145732
  18.3 57.3 %copy-start.2 = (s32[16]{0:T(128)S(1)}, s32[16]{0:T(128)}, u32[]{:S(2)}) copy-start(s32[16]{0:T(128)} %offsets.1) | copy-start | bytes 196
  21.3 62.2 %copy-start.1 = (bf16[288,256]{1,0:T(8,128)(2,1)S(1)}, bf16[288,256]{1,0:T(8,128)(2,1)}, u32[]{:S(2)}) copy-start(bf16[288,256]{1,0:T(8,128)(2,1)} %constant.56.clone.table) | copy-start | bytes 442372
  31.7 25.7 %all-to-all-start.1 = ((bf16[32,32,128]{2,1,0:T(8,128)(2,1)}), bf16[32,32,128]{2,1,0:T(8,128)(2,1)S(1)}, u32[]{:S(2)}, u32[]{:S(2)}) async-start(bf16[32,32,128]{2,1,0:T(8,128)(2,1)} %broadcast_in_dim.89), calls=%async_computation.1 | async-start | bytes 524288 | tf_op jit(solution)/shard_map/all_to_all | solution.py:271
  46.4 22.5 %collective-permute-start.1 = (bf16[8,256,128]{2,1,0:T(8,128)(2,1)S(1)}, bf16[8,256,128]{2,1,0:T(8,128)(2,1)S(1)}, u32[]{:S(2)}, u32[]{:S(2)}) collective-permute-start(bf16[8,256,128]{2,1,0:T(8,128)(2,1)S(1)} %get-tuple-element.4.own.white), channel_id=1, source_target_pairs={{2,0},{3,1},{4,2},{5,3},{6,4},{7,5},{8,6},{9,7},{10,8},{11,9},{12,... | collective-permute-start | bytes 1572872 | tf_op jit(solution)/shard_map/ppermute | solution.py:255
  48.6 27.1 %collective-permute-start = (bf16[8,256,128]{2,1,0:T(8,128)(2,1)S(1)}, bf16[8,256,128]{2,1,0:T(8,128)(2,1)S(1)}, u32[]{:S(2)}, u32[]{:S(2)}) collective-permute-start(bf16[8,256,128]{2,1,0:T(8,128)(2,1)S(1)} %get-tuple-element.4.own.white), channel_id=1, source_target_pairs={{1,0},{2,1},{3,2},{4,3},{5,4},{6,5},{7,6},{8,7},{9,8},{10,9},{11,1... | collective-permute-start | bytes 1572872 | tf_op jit(solution)/shard_map/ppermute | solution.py:255
  58.2 25.3 %all-to-all-start.2 = ((bf16[16,32,128]{2,1,0:T(8,128)(2,1)}), bf16[16,32,128]{2,1,0:T(8,128)(2,1)S(1)}, u32[]{:S(2)}, u32[]{:S(2)}) async-start(bf16[16,32,128]{2,1,0:T(8,128)(2,1)} %broadcast_in_dim.90), calls=%async_computation.2 | async-start | bytes 262144 | tf_op jit(solution)/shard_map/all_to_all | solution.py:274

commit v2 on v1

--- a/solution.py
+++ b/solution.py
@@ -22,6 +22,7 @@
 WIDTH = 128
 HALO = 16
 SPAN = 2 * NFFT + HALO
+SPAN_LANES = 640
 CHUNK = 16
 CHUNKS = NBIN // CHUNK
 VMEM_LIMIT = 48 * 1024 * 1024
@@ -44,26 +45,6 @@
     return np.concatenate([high, low], axis=0)
 
 
-def split(x, parts):
-    out = []
-    for _ in range(parts):
-        piece = lax.reduce_precision(x, 8, 7)
-        out.append(piece.astype(BF16))
-        x = x - piece
-    return out
-
-
-def filtered_table(taps):
-    n = lax.broadcasted_iota(jnp.int32, (NFFT, SPAN), 0)
-    i = lax.broadcasted_iota(jnp.int32, (NFFT, SPAN), 1)
-    which = 2 * n + HALO - i
-    spread = jnp.zeros((NFFT, SPAN), F32)
-    for j in range(TAPS):
-        spread = jnp.where(which == j, taps[j], spread)
-    table = jnp.dot(jnp.asarray(dft_table()), spread, precision=lax.Precision.HIGHEST)
-    return jnp.stack(split(table, 3))
-
-
 def chunk_rows(white, c):
     rows = []
     for f in range(FRAMES):
@@ -73,61 +54,109 @@
     return rows
 
 
-def whiten_kernel(table, raw, mask, counts, onehot, white, picked, spectrum):
+def band_masks(edges):
+    band = lax.broadcasted_iota(jnp.int32, (BANDS, NBIN), 0)
+    bins = lax.broadcasted_iota(jnp.int32, (BANDS, NBIN), 1)
+    lowest = jnp.zeros((BANDS, NBIN), jnp.int32)
+    limit = jnp.zeros((BANDS, NBIN), jnp.int32)
+    for b in range(BANDS):
+        lowest = jnp.where(band == b, edges[b], lowest)
+        limit = jnp.where(band == b, edges[b + 1], limit)
+    mask = jnp.where((bins >= lowest) & (bins < limit), 1.0, 0.0).astype(F32)
+    return mask, (limit - lowest).astype(F32)
+
+
+def filtered_table(taps, dft, spread, table):
+    rows = 32
+    spread[...] = jnp.zeros((NFFT, SPAN_LANES), F32)
+    for start in range(0, NFFT, rows):
+        left = (2 * start + 1) // WIDTH * WIDTH
+        n = start + lax.broadcasted_iota(jnp.int32, (rows, 2 * WIDTH), 0)
+        i = left + lax.broadcasted_iota(jnp.int32, (rows, 2 * WIDTH), 1)
+        which = 2 * n + HALO - i
+        block = jnp.zeros((rows, 2 * WIDTH), F32)
+        for j in range(TAPS):
+            block = jnp.where(which == j, taps[j], block)
+        spread[start : start + rows, left : left + 2 * WIDTH] = block
+    rest = jnp.dot(dft[...], spread[...], precision=lax.Precision.HIGHEST)
+    for part in range(3):
+        piece = rest.astype(BF16)
+        table[part] = piece
+        rest = rest - piece.astype(F32)
+
+
+def whiten_kernel(first, taps, edges, sources, dft, raw, white, picked, spread, table, spectrum):
+    filtered_table(taps, dft, spread, table)
     squares = jnp.zeros((NFFT, WIDTH), F32)
     for f in range(FRAMES):
         total = jnp.zeros((NFFT, WIDTH), F32)
         for part in range(3):
             if f == 0:
                 total += jnp.dot(
-                    table[part, :, HALO:], raw[: 2 * NFFT, :], preferred_element_type=F32
+                    table[part, :, HALO:SPAN], raw[: 2 * NFFT, :], preferred_element_type=F32
                 )
             else:
                 start = f * 2 * NFFT - HALO
                 total += jnp.dot(
-                    table[part], raw[start : start + SPAN, :], preferred_element_type=F32
+                    table[part, :, :SPAN], raw[start : start + SPAN, :], preferred_element_type=F32
                 )
         spectrum[f] = total
         squares += total * total
     squares = squares[:NBIN] + squares[NBIN:]
-    power = jnp.dot(mask[...], squares, precision=lax.Precision.HIGHEST) / counts[...]
+    mask, bins = band_masks(edges)
+    power = jnp.dot(mask, squares, precision=lax.Precision.HIGHEST) / (2.0 * FRAMES * bins)
     level = jnp.sqrt(power + 1e-06)
     per_bin = lax.dot_general(
-        mask[...], level, (((0,), (0,)), ((), ())), precision=lax.Precision.HIGHEST
+        mask, level, (((0,), (0,)), ((), ())), precision=lax.Precision.HIGHEST
     )
     inverse = 1.0 / per_bin
     for f in range(FRAMES):
         white[f, :NBIN, :] = (spectrum[f, :NBIN, :] * inverse).astype(BF16)
         white[f, NBIN:, :] = (spectrum[f, NBIN:, :] * inverse).astype(BF16)
+    which = lax.broadcasted_iota(jnp.int32, (SOURCES, WIDTH), 0)
+    channel = first[0] + lax.broadcasted_iota(jnp.int32, (SOURCES, WIDTH), 1)
+    wanted = jnp.zeros((SOURCES, WIDTH), jnp.int32)
+    for s in range(SOURCES):
+        wanted = jnp.where(which == s, sources[s], wanted)
+    onehot = jnp.where(wanted == channel, 1.0, 0.0).astype(BF16)
     for c in range(CHUNKS):
         rows = jnp.concatenate(chunk_rows(white, c), axis=0)
         found = lax.dot_general(
-            onehot[...], rows, (((1,), (1,)), ((), ())), preferred_element_type=F32
+            onehot, rows, (((1,), (1,)), ((), ())), preferred_element_type=F32
         ).astype(BF16)
         picked[2 * c] = found[:, :WIDTH]
         picked[2 * c + 1] = found[:, WIDTH:]
 
 
-def whiten(raw, taps, mask, onehot):
-    counts = 2.0 * FRAMES * jnp.sum(mask, axis=1, keepdims=True)
+SMEM = pl.BlockSpec(memory_space=pltpu.SMEM)
+VMEM = pl.BlockSpec(memory_space=pltpu.VMEM)
+
+
+def whiten(raw, taps, edges, sources, first):
     return pl.pallas_call(
         whiten_kernel,
         out_shape=(
             jax.ShapeDtypeStruct((FRAMES, NFFT, WIDTH), BF16),
             jax.ShapeDtypeStruct((2 * CHUNKS, SOURCES, WIDTH), BF16),
         ),
-        scratch_shapes=[pltpu.VMEM((FRAMES, NFFT, WIDTH), F32)],
+        in_specs=[SMEM] * 4 + [VMEM] * 2,
+        out_specs=(VMEM, VMEM),
+        scratch_shapes=[
+            pltpu.VMEM((NFFT, SPAN_LANES), F32),
+            pltpu.VMEM((3, NFFT, SPAN_LANES), BF16),
+            pltpu.VMEM((FRAMES, NFFT, WIDTH), F32),
+        ],
         compiler_params=pltpu.CompilerParams(vmem_limit_bytes=VMEM_LIMIT),
         name="whiten",
-    )(filtered_table(taps), raw, mask, counts, onehot)
-
-
-def coherence_kernel(offsets, mask, scale, own, near, far, out, ext, base, high, low):
+    )(first, taps, edges, sources, jnp.asarray(dft_table()), raw)
+
+
+def coherence_kernel(offsets, edges, own, near, far, out, ext, base, high, low):
     for f in range(FRAMES):
         base[f] = own[f].astype(F32)
-        ext[0, f] = base[f]
-        ext[1, f] = near[f].astype(F32)
-        ext[2, f] = far[f].astype(F32)
+        ext[0, f] = own[f]
+        ext[1, f] = near[f]
+        ext[2, f] = far[f]
     lane = lax.broadcasted_iota(jnp.int32, (1, WIDTH), 1)
     step = 32
 
@@ -142,7 +171,7 @@
         def partner(f, start):
             a = ext[first, f, start : start + step, :]
             b = ext[second, f, start : start + step, :]
-            return pltpu.roll(jnp.where(wrapped, b, a), shift, 1)
+            return pltpu.roll(jnp.where(wrapped, b, a), shift, 1).astype(F32)
 
         for k in range(0, NBIN, step):
             real = jnp.zeros((step, WIDTH), F32)
@@ -160,34 +189,34 @@
         return 0
 
     lax.fori_loop(0, OFFS, pair, 0)
-    bands = mask[...].astype(BF16)
+    mask, bins = band_masks(edges)
+    scale = 1.0 / jnp.sqrt(FRAMES * bins)
+    bands = mask.astype(BF16)
     for p in range(OFFS):
         for part in range(2):
             total = jnp.dot(bands, high[p, part], preferred_element_type=F32)
             total += jnp.dot(bands, low[p, part], preferred_element_type=F32)
-            out[p, part * BANDS : (part + 1) * BANDS, :] = total * scale[...]
-
-
-def coherences(offsets, mask, own, near, far):
-    scale = 1.0 / jnp.sqrt(FRAMES * jnp.sum(mask, axis=1, keepdims=True))
-    vmem = pl.BlockSpec(memory_space=pltpu.VMEM)
+            out[p, part * BANDS : (part + 1) * BANDS, :] = total * scale
+
+
+def coherences(offsets, edges, own, near, far):
     return pl.pallas_call(
         coherence_kernel,
         out_shape=jax.ShapeDtypeStruct((OFFS, 2 * BANDS, WIDTH), F32),
-        in_specs=[pl.BlockSpec(memory_space=pltpu.SMEM)] + [vmem] * 5,
-        out_specs=vmem,
+        in_specs=[SMEM] * 2 + [VMEM] * 3,
+        out_specs=VMEM,
         scratch_shapes=[
-            pltpu.VMEM((3, FRAMES, NFFT, WIDTH), F32),
+            pltpu.VMEM((3, FRAMES, NFFT, WIDTH), BF16),
             pltpu.VMEM((FRAMES, NFFT, WIDTH), F32),
             pltpu.VMEM((OFFS, 2, NBIN, WIDTH), BF16),
             pltpu.VMEM((OFFS, 2, NBIN, WIDTH), BF16),
         ],
         compiler_params=pltpu.CompilerParams(vmem_limit_bytes=VMEM_LIMIT),
         name="coherence",
-    )(offsets, mask, scale, own, near, far)
-
-
-S_STEP = 4
+    )(offsets, edges, own, near, far)
+
+
+S_STEP = 8
 
 
 def correlate_kernel(table, sources, white, out, left, high, low):
@@ -224,21 +253,21 @@
         both = jnp.dot(table[...], top, preferred_element_type=F32)
         lagged = both[:LAG_ROWS] + both[LAG_ROWS:]
         lagged += jnp.dot(table[:LAG_ROWS, :], rest, preferred_element_type=F32)
-        out[i] = lagged[:LAGS, :WIDTH]
-        out[i + 1] = lagged[:LAGS, WIDTH:]
+        out[:, i, :] = lagged[:LAGS, :WIDTH]
+        out[:, i + 1, :] = lagged[:LAGS, WIDTH:]
 
 
 def correlations(sources, white):
     return pl.pallas_call(
         correlate_kernel,
         grid=(SOURCES // S_STEP,),
-        out_shape=jax.ShapeDtypeStruct((SOURCES, LAGS, WIDTH), F32),
+        out_shape=jax.ShapeDtypeStruct((LAGS, SOURCES, WIDTH), F32),
         in_specs=[
             pl.BlockSpec((2 * LAG_ROWS, NFFT), lambda g: (0, 0)),
             pl.BlockSpec((2 * CHUNKS, SOURCES, WIDTH), lambda g: (0, 0, 0)),
             pl.BlockSpec((FRAMES, NFFT, WIDTH), lambda g: (0, 0, 0)),
         ],
-        out_specs=pl.BlockSpec((S_STEP, LAGS, WIDTH), lambda g: (g, 0, 0)),
+        out_specs=pl.BlockSpec((LAGS, S_STEP, WIDTH), lambda g: (0, g, 0)),
         scratch_shapes=[
             pltpu.VMEM((SOURCES * CHUNK, NFFT), BF16),
             pltpu.VMEM((SOURCES, NFFT, WIDTH), BF16),
@@ -246,7 +275,7 @@
         ],
         compiler_params=pltpu.CompilerParams(vmem_limit_bytes=VMEM_LIMIT),
         name="correlate",
-    )(jnp.asarray(lag_tables()), sources, white)
+    )(jnp.asarray(lag_tables()), sources, white).transpose(1, 0, 2)
 
 
 def from_behind(block, axis, distance):
@@ -275,14 +304,11 @@
 
 
 def per_device(raw, taps, offsets, sources, edges):
-    bins = jnp.arange(NBIN, dtype=jnp.int32)
-    mask = ((bins[None, :] >= edges[:-1, None]) & (bins[None, :] < edges[1:, None])).astype(F32)
-    owned = lax.axis_index("ch") * WIDTH + jnp.arange(WIDTH, dtype=jnp.int32)
-    onehot = (sources[:, None] == owned[None, :]).astype(BF16)
-    white, picked = whiten(raw, taps, mask, onehot)
+    first = jnp.full((1,), lax.axis_index("ch") * WIDTH, jnp.int32)
+    white, picked = whiten(raw, taps, edges, sources, first)
     near = from_behind(white, "ch", -1)
     far = from_behind(white, "ch", -2)
-    coherence = coherences(offsets, mask, white, near, far)
+    coherence = coherences(offsets, edges, white, near, far)
     correlation = correlations(spread_sources(picked), white)
     return (coherence, correlation)
 

time: 88.8 us -> 75.1 us (0.85)
  matrix products: 12.6 us -> 0 us
  Pallas kernels: 13.9 us -> 15.5 us
  local copies, waits for them, and re-layouts: 7.1 us -> 5.57 us
  other arithmetic: 1.24 us -> 0.08 us
    dot_general x1 -> x0, matrix products: 12.6 us -> none  [filtered_table(): jnp.dot(jnp.asarray(dft_table()), spread, precision=lax.Precision.HIGHEST)]
    slice x2 -> x0, local copies, waits for them, and re-layouts: 2.76 us -> none  [the longest x1 1.96 us: filtered_table(): spread = jnp.where(which == j, taps[j], spread)]
    pallas_call x1, Pallas kernels: 2.98 us -> 4.91 us  [whiten(): pl.pallas_call(whiten_kernel, out_shape=(jax.ShapeDtypeStruct((FRAMES, NF...]
    unnamed x7 -> x16, local copies, waits for them, and re-layouts: 2.75 us -> 4.15 us
    pallas_call x1, Pallas kernels: 7.84 us -> 6.59 us  [coherences(): pl.pallas_call(coherence_kernel, out_shape=jax.ShapeDtypeStruct((OFFS, 2...]
    pallas_call x1, Pallas kernels: 3.04 us -> 3.99 us  [correlations(): pl.pallas_call(correlate_kernel, grid=(SOURCES // S_STEP,), out_shape=jax...]
where the time goes in v2:
time: 75.1 us; the launch traced here: 74.6 us
  starting transfers between devices  29.3 us (39%)
  Pallas kernels  15.5 us (21%)
  waiting for transfers between devices  13.8 us (18%)
  blocking collectives  9.66 us (13%)
  local copies, waits for them, and re-layouts  5.57 us (7%)
    all_to_all x1, starting transfers between devices, spread_sources(): lax.all_to_all(copies, 'ch', 0, 0, axis_index_groups=places, tiled=True)  14.6 us
    all_to_all x1, blocking collectives, spread_sources(): lax.all_to_all(picked, 'ch', 0, 0, axis_index_groups=runs, tiled=True)  9.66 us
    all_to_all x1, starting transfers between devices, spread_sources(): lax.all_to_all(copies, 'ch', 0, 0, axis_index_groups=runs, tiled=True)  9.42 us
    ppermute x2, waiting for transfers between devices, from_behind(): return lax.ppermute(block, axis, route)  8 us
    pallas_call x1, Pallas kernels, coherences(): pl.pallas_call(coherence_kernel, out_shape=jax.ShapeDtypeStruct((OFFS, 2...  6.59 us
    all_to_all x1, waiting for transfers between devices, spread_sources(): lax.all_to_all(copies, 'ch', 0, 0, axis_index_groups=places, tiled=True)  5.82 us
    ppermute x2, starting transfers between devices, from_behind(): return lax.ppermute(block, axis, route)  5.28 us
    pallas_call x1, Pallas kernels, whiten(): pl.pallas_call(whiten_kernel, out_shape=(jax.ShapeDtypeStruct((FRAMES, NF...  4.91 us
  transfers between devices with their start and end apart: 4, of which 3 were waited for; matrix products, arithmetic and copies ran while one was open for 1% of the time, Pallas kernels for 9%

profile of v2, /device:TPU:31, one launch (start us, length us, event | category | flops | bytes accessed | tf_op | source)
XLA Modules:
  0.0 74.6 jit_solution(1627423770341174529)
XLA Ops:
  0.6 0.0 copy-start.4
  0.6 0.0 copy-start.7
  0.7 0.0 copy-start
  0.7 1.2 %copy-done = bf16[4096,128]{1,0:T(8,128)(2,1)S(1)} copy-done((bf16[4096,128]{1,0:T(8,128)(2,1)S(1)}, bf16[4096,128]{1,0:T(8,128)(2,1)}, u32[]{:S(2)}) %copy-start) | copy-done | bytes 1048600
  1.9 0.0 copy-start.1
  1.9 0.9 %copy-done.1 = f32[256,256]{1,0:T(8,128)S(1)} copy-done((f32[256,256]{1,0:T(8,128)S(1)}, f32[256,256]{1,0:T(8,128)}, u32[]{:S(2)}) %copy-start.1) | copy-done | bytes 262168
  2.8 0.0 copy-start.3
  2.8 0.7 copy-done.3
  3.5 0.0 copy-start.5
  3.5 0.7 copy-done.5
  4.2 0.0 copy-start.6
  4.2 0.7 copy-done.6
  4.8 4.9 %whiten.1 = (bf16[8,256,128]{2,1,0:T(8,128)(2,1)S(1)}, bf16[16,32,128]{2,1,0:T(8,128)(2,1)S(1)}) custom-call(s32[1]{0:T(128)} %bitcast.first, f32[16]{0:T(128)S(1)} %copy-done.5, s32[17]{0:T(128)S(1)} %copy-done.3, s32[32]{0:T(128)S(1)} %copy-done.6, f32[256,256]{1,0:T(8,128)S(1)} %copy-done.1, bf16[4096,128]{1,0:T(8,128)(2,1)S(1)} %copy-done), custom_call_target="tpu_custom_call" | custom-call | tf_op jit(solution)/shard_map/whiten/pallas_call | solution.py:136
  9.7 0.0 copy-start.2
  9.7 9.7 %all_to_all.15 = bf16[16,32,128]{2,1,0:T(8,128)(2,1)S(1)} all-to-all(bf16[16,32,128]{2,1,0:T(8,128)(2,1)S(1)} %get-tuple-element.5), channel_id=1, replica_groups={{0,1,2,3,4,5,6,7,8,9,10,11,12,13,14,15},{16,17,18,19,20,21,22,23,24,25,..., dimensions={0} | all-to-all | bytes 262144 | tf_op jit(solution)/shard_map/all_to_all | solution.py:297
  19.4 0.7 broadcast_in_dim.7
  20.2 14.6 %all-to-all-start.1 = ((bf16[32,32,128]{2,1,0:T(8,128)(2,1)}), bf16[32,32,128]{2,1,0:T(8,128)(2,1)S(1)}, u32[]{:S(2)}, u32[]{:S(2)}) async-start(bf16[32,32,128]{2,1,0:T(8,128)(2,1)} %broadcast_in_dim.7), calls=%async_computation.1 | async-start | bytes 524288 | tf_op jit(solution)/shard_map/all_to_all | solution.py:300
  34.8 2.2 %collective-permute-start.1 = (bf16[8,256,128]{2,1,0:T(8,128)(2,1)S(1)}, bf16[8,256,128]{2,1,0:T(8,128)(2,1)S(1)}, u32[]{:S(2)}, u32[]{:S(2)}) collective-permute-start(bf16[8,256,128]{2,1,0:T(8,128)(2,1)S(1)} %get-tuple-element.4.own.white), channel_id=1, source_target_pairs={{2,0},{3,1},{4,2},{5,3},{6,4},{7,5},{8,6},{9,7},{10,8},{11,9},{12,... | collective-permute-start | bytes 1572872 | tf_op jit(solution)/shard_map/ppermute | solution.py:284
  37.0 3.1 %collective-permute-start = (bf16[8,256,128]{2,1,0:T(8,128)(2,1)S(1)}, bf16[8,256,128]{2,1,0:T(8,128)(2,1)S(1)}, u32[]{:S(2)}, u32[]{:S(2)}) collective-permute-start(bf16[8,256,128]{2,1,0:T(8,128)(2,1)S(1)} %get-tuple-element.4.own.white), channel_id=1, source_target_pairs={{1,0},{2,1},{3,2},{4,3},{5,4},{6,5},{7,6},{8,7},{9,8},{10,9},{11,1... | collective-permute-start | bytes 1572872 | tf_op jit(solution)/shard_map/ppermute | solution.py:284
  40.1 5.8 %all-to-all-done.1 = bf16[32,32,128]{2,1,0:T(8,128)(2,1)S(1)} async-done(((bf16[32,32,128]{2,1,0:T(8,128)(2,1)}), bf16[32,32,128]{2,1,0:T(8,128)(2,1)S(1)}, u32[]{:S(2)}, u32[]{:S(2)}) %all-to-all-start.1) | async-done | bytes 262176 | tf_op jit(solution)/shard_map/all_to_all | solution.py:300
  45.9 0.1 reduce_sum.25
  45.9 0.7 broadcast_in_dim.8
  46.6 9.4 %all-to-all-start.2 = ((bf16[16,32,128]{2,1,0:T(8,128)(2,1)}), bf16[16,32,128]{2,1,0:T(8,128)(2,1)S(1)}, u32[]{:S(2)}, u32[]{:S(2)}) async-start(bf16[16,32,128]{2,1,0:T(8,128)(2,1)} %broadcast_in_dim.8), calls=%async_computation.2 | async-start | bytes 262144 | tf_op jit(solution)/shard_map/all_to_all | solution.py:303
  56.0 1.2 %collective-permute-done.1.far = bf16[8,256,128]{2,1,0:T(8,128)(2,1)S(1)} collective-permute-done((bf16[8,256,128]{2,1,0:T(8,128)(2,1)S(1)}, bf16[8,256,128]{2,1,0:T(8,128)(2,1)S(1)}, u32[]{:S(2)}, u32[]{:S(2)}) %collective-permute-start.1) | collective-permute-done | bytes 524320 | tf_op jit(solution)/shard_map/ppermute | solution.py:284
  57.3 6.8 %collective-permute-done.near = bf16[8,256,128]{2,1,0:T(8,128)(2,1)S(1)} collective-permute-done((bf16[8,256,128]{2,1,0:T(8,128)(2,1)S(1)}, bf16[8,256,128]{2,1,0:T(8,128)(2,1)S(1)}, u32[]{:S(2)}, u32[]{:S(2)}) %collective-permute-start) | collective-permute-done | bytes 524320 | tf_op jit(solution)/shard_map/ppermute | solution.py:284
  64.1 0.0 copy-done.4
  64.1 0.0 copy-done.7
  64.1 6.6 %coherence.1 = f32[16,32,128]{2,1,0:T(8,128)} custom-call(s32[16]{0:T(128)S(1)} %copy-done.7, s32[17]{0:T(128)S(1)} %copy-done.4, bf16[8,256,128]{2,1,0:T(8,128)(2,1)S(1)} %get-tuple-element.4.own.white, bf16[8,256,128]{2,1,0:T(8,128)(2,1)S(1)} %collective-permute-done.near, bf16[8,256,128]{2,1,0:T(8,128)(2,1)S(1)} %collective-permute-done.1.far), custom_call_target="tpu_custom_call" | custom-call | tf_op jit(solution)/shard_map/coherence/pallas_call | solution.py:203
  70.7 0.0 all-to-all-done.2.sources
  70.7 0.0 copy-done.2
  70.7 4.0 %correlate.1 = f32[129,32,128]{2,1,0:T(8,128)} custom-call(bf16[288,256]{1,0:T(8,128)(2,1)S(1)} %copy-done.2, bf16[16,32,128]{2,1,0:T(8,128)(2,1)S(1)} %all-to-all-done.2.sources, bf16[8,256,128]{2,1,0:T(8,128)(2,1)S(1)} %get-tuple-element.4.own.white), custom_call_target="tpu_custom_call" | custom-call | tf_op jit(solution)/shard_map/correlate/pallas_call | solution.py:261
  (1 shorter events, 0.0 us)
Async XLA Ops:
  0.6 63.4 %copy-start.4 = (s32[17]{0:T(128)S(1)}, s32[17]{0:T(128)}, u32[]{:S(2)}) copy-start(s32[17]{0:T(128)} %edges.3) | copy-start | bytes 208
  0.6 63.4 %copy-start.7 = (s32[16]{0:T(128)S(1)}, s32[16]{0:T(128)}, u32[]{:S(2)}) copy-start(s32[16]{0:T(128)} %offsets.1) | copy-start | bytes 196
  0.7 1.2 %copy-start = (bf16[4096,128]{1,0:T(8,128)(2,1)S(1)}, bf16[4096,128]{1,0:T(8,128)(2,1)}, u32[]{:S(2)}) copy-start(bf16[4096,128]{1,0:T(8,128)(2,1)} %raw.1) | copy-start | bytes 3145732
  1.9 0.9 %copy-start.1 = (f32[256,256]{1,0:T(8,128)S(1)}, f32[256,256]{1,0:T(8,128)}, u32[]{:S(2)}) copy-start(f32[256,256]{1,0:T(8,128)} %constant.14.clone.dft) | copy-start | bytes 786436
  2.8 0.7 copy-start.3
  3.5 0.7 copy-start.5
  4.2 0.7 copy-start.6
  9.7 60.9 %copy-start.2 = (bf16[288,256]{1,0:T(8,128)(2,1)S(1)}, bf16[288,256]{1,0:T(8,128)(2,1)}, u32[]{:S(2)}) copy-start(bf16[288,256]{1,0:T(8,128)(2,1)} %constant.15.clone.table) | copy-start | bytes 442372
  20.2 25.7 %all-to-all-start.1 = ((bf16[32,32,128]{2,1,0:T(8,128)(2,1)}), bf16[32,32,128]{2,1,0:T(8,128)(2,1)S(1)}, u32[]{:S(2)}, u32[]{:S(2)}) async-start(bf16[32,32,128]{2,1,0:T(8,128)(2,1)} %broadcast_in_dim.7), calls=%async_computation.1 | async-start | bytes 524288 | tf_op jit(solution)/shard_map/all_to_all | solution.py:300
  34.8 22.5 %collective-permute-start.1 = (bf16[8,256,128]{2,1,0:T(8,128)(2,1)S(1)}, bf16[8,256,128]{2,1,0:T(8,128)(2,1)S(1)}, u32[]{:S(2)}, u32[]{:S(2)}) collective-permute-start(bf16[8,256,128]{2,1,0:T(8,128)(2,1)S(1)} %get-tuple-element.4.own.white), channel_id=1, source_target_pairs={{2,0},{3,1},{4,2},{5,3},{6,4},{7,5},{8,6},{9,7},{10,8},{11,9},{12,... | collective-permute-start | bytes 1572872 | tf_op jit(solution)/shard_map/ppermute | solution.py:284
  37.0 27.1 %collective-permute-start = (bf16[8,256,128]{2,1,0:T(8,128)(2,1)S(1)}, bf16[8,256,128]{2,1,0:T(8,128)(2,1)S(1)}, u32[]{:S(2)}, u32[]{:S(2)}) collective-permute-start(bf16[8,256,128]{2,1,0:T(8,128)(2,1)S(1)} %get-tuple-element.4.own.white), channel_id=1, source_target_pairs={{1,0},{2,1},{3,2},{4,3},{5,4},{6,5},{7,6},{8,7},{9,8},{10,9},{11,1... | collective-permute-start | bytes 1572872 | tf_op jit(solution)/shard_map/ppermute | solution.py:284
  46.6 24.0 %all-to-all-start.2 = ((bf16[16,32,128]{2,1,0:T(8,128)(2,1)}), bf16[16,32,128]{2,1,0:T(8,128)(2,1)S(1)}, u32[]{:S(2)}, u32[]{:S(2)}) async-start(bf16[16,32,128]{2,1,0:T(8,128)(2,1)} %broadcast_in_dim.8), calls=%async_computation.2 | async-start | bytes 262144 | tf_op jit(solution)/shard_map/all_to_all | solution.py:303

commit v3 on v2

--- a/solution.py
+++ b/solution.py
@@ -25,14 +25,20 @@
 SPAN_LANES = 640
 CHUNK = 16
 CHUNKS = NBIN // CHUNK
+RUN = 16
 VMEM_LIMIT = 48 * 1024 * 1024
 F32 = jnp.float32
 BF16 = jnp.bfloat16
 
 
-def dft_table():
-    phase = np.arange(NBIN)[:, None] * np.arange(NFFT)[None, :] % NFFT * (2.0 * math.pi / NFFT)
-    return np.concatenate([np.cos(phase), -np.sin(phase)], axis=0).astype(np.float32)
+def turn_tables():
+    sample = np.arange(SPAN)[None, :] - HALO
+    bins = np.arange(NBIN)[:, None]
+    phase = bins * sample % (2 * NFFT) * (math.pi / NFFT)
+    turns = np.stack([np.cos(phase), np.sin(phase)]).astype(np.float32)
+    turns = np.pad(turns, ((0, 0), (0, 0), (0, SPAN_LANES - SPAN)))
+    phase = bins * np.arange(TAPS)[None, :] % (2 * NFFT) * (math.pi / NFFT)
+    return turns, np.concatenate([np.cos(phase), -np.sin(phase)], axis=0).astype(np.float32)
 
 
 def lag_tables():
@@ -66,42 +72,72 @@
     return mask, (limit - lowest).astype(F32)
 
 
-def filtered_table(taps, dft, spread, table):
-    rows = 32
-    spread[...] = jnp.zeros((NFFT, SPAN_LANES), F32)
-    for start in range(0, NFFT, rows):
-        left = (2 * start + 1) // WIDTH * WIDTH
-        n = start + lax.broadcasted_iota(jnp.int32, (rows, 2 * WIDTH), 0)
-        i = left + lax.broadcasted_iota(jnp.int32, (rows, 2 * WIDTH), 1)
-        which = 2 * n + HALO - i
-        block = jnp.zeros((rows, 2 * WIDTH), F32)
-        for j in range(TAPS):
-            block = jnp.where(which == j, taps[j], block)
-        spread[start : start + rows, left : left + 2 * WIDTH] = block
-    rest = jnp.dot(dft[...], spread[...], precision=lax.Precision.HIGHEST)
-    for part in range(3):
-        piece = rest.astype(BF16)
-        table[part] = piece
-        rest = rest - piece.astype(F32)
-
-
-def whiten_kernel(first, taps, edges, sources, dft, raw, white, picked, spread, table, spectrum):
-    filtered_table(taps, dft, spread, table)
+def filtered_table(taps, turns, tap_turns, table):
+    tap = lax.broadcasted_iota(jnp.int32, (TAPS, WIDTH), 0)
+    lane = lax.broadcasted_iota(jnp.int32, (TAPS, WIDTH), 1)
+    value = jnp.zeros((TAPS, WIDTH), F32)
+    for j in range(TAPS):
+        value = jnp.where(tap == j, taps[j], value)
+    value = jnp.where((lane + tap) % 2 == 0, value, 0.0)
+    early = jnp.where(lane + tap >= HALO, value, 0.0)
+    late = jnp.where(lane + tap < HALO, value, 0.0)
+    meets = jnp.concatenate([early, value, late], axis=1)
+    response = jnp.dot(tap_turns[...], meets, precision=lax.Precision.HIGHEST)
+    for block in range(SPAN_LANES // WIDTH):
+        lanes = slice(block * WIDTH, (block + 1) * WIDTH)
+        kind = 0 if block == 0 else 2 if block == SPAN_LANES // WIDTH - 1 else 1
+        re = response[:NBIN, kind * WIDTH : (kind + 1) * WIDTH]
+        im = response[NBIN:, kind * WIDTH : (kind + 1) * WIDTH]
+        cos, sin = turns[0, :, lanes], turns[1, :, lanes]
+        for half, rest in enumerate((cos * re + sin * im, cos * im - sin * re)):
+            for part in range(3):
+                piece = rest.astype(BF16)
+                row = part * NFFT + half * NBIN
+                table[row : row + NBIN, lanes] = piece
+                rest = rest - piece.astype(F32)
+
+
+def whiten_kernel(
+    first, taps_hbm, edges_hbm, sources_hbm, turns_hbm, tap_turns_hbm, raw_hbm,
+    white, picked,
+    taps, edges, sources, turns, tap_turns, raw, table, spectrum, sems,
+):
+    loads = [
+        pltpu.make_async_copy(src, dst, sems.at[i])
+        for i, (src, dst) in enumerate(
+            (
+                (taps_hbm, taps),
+                (tap_turns_hbm, tap_turns),
+                (turns_hbm, turns),
+                (raw_hbm, raw),
+                (edges_hbm, edges),
+                (sources_hbm, sources),
+            )
+        )
+    ]
+    for load in loads:
+        load.start()
+    for load in loads[:3]:
+        load.wait()
+    filtered_table(taps, turns, tap_turns, table)
+    for load in loads[3:]:
+        load.wait()
     squares = jnp.zeros((NFFT, WIDTH), F32)
-    for f in range(FRAMES):
-        total = jnp.zeros((NFFT, WIDTH), F32)
-        for part in range(3):
-            if f == 0:
-                total += jnp.dot(
-                    table[part, :, HALO:SPAN], raw[: 2 * NFFT, :], preferred_element_type=F32
-                )
-            else:
-                start = f * 2 * NFFT - HALO
-                total += jnp.dot(
-                    table[part, :, :SPAN], raw[start : start + SPAN, :], preferred_element_type=F32
-                )
-        spectrum[f] = total
-        squares += total * total
+    halo = [jnp.zeros((HALO, WIDTH), BF16)]
+    halo += [raw[f * 2 * NFFT - HALO : f * 2 * NFFT, :] for f in range(1, FRAMES)]
+    for f in range(0, FRAMES, 2):
+        pair = [
+            jnp.concatenate([halo[g], raw[g * 2 * NFFT : (g + 1) * 2 * NFFT, :]], axis=0)
+            for g in (f, f + 1)
+        ]
+        parts = jnp.dot(
+            table[:, :SPAN], jnp.concatenate(pair, axis=1), preferred_element_type=F32
+        )
+        both = parts[:NFFT] + parts[NFFT : 2 * NFFT] + parts[2 * NFFT :]
+        for g in range(2):
+            total = both[:, g * WIDTH : (g + 1) * WIDTH]
+            spectrum[f + g] = total
+            squares += total * total
     squares = squares[:NBIN] + squares[NBIN:]
     mask, bins = band_masks(edges)
     power = jnp.dot(mask, squares, precision=lax.Precision.HIGHEST) / (2.0 * FRAMES * bins)
@@ -133,70 +169,82 @@
 
 
 def whiten(raw, taps, edges, sources, first):
+    turns, tap_turns = turn_tables()
     return pl.pallas_call(
         whiten_kernel,
         out_shape=(
             jax.ShapeDtypeStruct((FRAMES, NFFT, WIDTH), BF16),
             jax.ShapeDtypeStruct((2 * CHUNKS, SOURCES, WIDTH), BF16),
         ),
-        in_specs=[SMEM] * 4 + [VMEM] * 2,
+        in_specs=[SMEM] + [pl.BlockSpec(memory_space=pl.ANY)] * 6,
         out_specs=(VMEM, VMEM),
         scratch_shapes=[
-            pltpu.VMEM((NFFT, SPAN_LANES), F32),
-            pltpu.VMEM((3, NFFT, SPAN_LANES), BF16),
+            pltpu.SMEM((TAPS,), F32),
+            pltpu.SMEM((BANDS + 1,), jnp.int32),
+            pltpu.SMEM((SOURCES,), jnp.int32),
+            pltpu.VMEM((2, NBIN, SPAN_LANES), F32),
+            pltpu.VMEM((NFFT, TAPS), F32),
+            pltpu.VMEM((SAMPLES, WIDTH), BF16),
+            pltpu.VMEM((3 * NFFT, SPAN_LANES), BF16),
             pltpu.VMEM((FRAMES, NFFT, WIDTH), F32),
+            pltpu.SemaphoreType.DMA((6,)),
         ],
-        compiler_params=pltpu.CompilerParams(vmem_limit_bytes=VMEM_LIMIT),
         name="whiten",
-    )(first, taps, edges, sources, jnp.asarray(dft_table()), raw)
-
-
-def coherence_kernel(offsets, edges, own, near, far, out, ext, base, high, low):
+    )(first, taps, edges, sources, jnp.asarray(turns), jnp.asarray(tap_turns), raw)
+
+
+def coherence_kernel(offsets, edges, own, near, far, out, ext, high, low):
     for f in range(FRAMES):
-        base[f] = own[f].astype(F32)
         ext[0, f] = own[f]
         ext[1, f] = near[f]
         ext[2, f] = far[f]
     lane = lax.broadcasted_iota(jnp.int32, (1, WIDTH), 1)
-    step = 32
-
-    def pair(p, _):
-        offset = offsets[p]
+    step = 16
+
+    def place(offset):
         first = offset // WIDTH
-        second = jnp.minimum(first + 1, 2)
         turn = offset % WIDTH
         wrapped = jnp.broadcast_to(lane < turn, (step, WIDTH))
-        shift = (WIDTH - turn) % WIDTH
-
-        def partner(f, start):
-            a = ext[first, f, start : start + step, :]
-            b = ext[second, f, start : start + step, :]
-            return pltpu.roll(jnp.where(wrapped, b, a), shift, 1).astype(F32)
-
+        return first, jnp.minimum(first + 1, 2), wrapped, (WIDTH - turn) % WIDTH
+
+    def partner(where, f, start):
+        first, second, wrapped, shift = where
+        a = ext[first, f, start : start + step, :]
+        b = ext[second, f, start : start + step, :]
+        return pltpu.roll(jnp.where(wrapped, b, a), shift, 1).astype(F32)
+
+    def pairs(i, _):
+        places = [place(offsets[4 * i + n]) for n in range(4)]
         for k in range(0, NBIN, step):
-            real = jnp.zeros((step, WIDTH), F32)
-            imag = jnp.zeros((step, WIDTH), F32)
+            real = [jnp.zeros((step, WIDTH), F32) for _ in places]
+            imag = [jnp.zeros((step, WIDTH), F32) for _ in places]
             for f in range(FRAMES):
-                p_re, p_im = partner(f, k), partner(f, NBIN + k)
-                w_re = base[f, k : k + step, :]
-                w_im = base[f, NBIN + k : NBIN + k + step, :]
-                real += w_re * p_re + w_im * p_im
-                imag += w_im * p_re - w_re * p_im
-            for part, cross in enumerate((real, imag)):
-                top = cross.astype(BF16)
-                high[p, part, k : k + step, :] = top
-                low[p, part, k : k + step, :] = (cross - top.astype(F32)).astype(BF16)
+                w_re = own[f, k : k + step, :].astype(F32)
+                w_im = own[f, NBIN + k : NBIN + k + step, :].astype(F32)
+                for n, where in enumerate(places):
+                    p_re, p_im = partner(where, f, k), partner(where, f, NBIN + k)
+                    real[n] += w_re * p_re + w_im * p_im
+                    imag[n] += w_im * p_re - w_re * p_im
+            for n in range(4):
+                for part, cross in enumerate((real[n], imag[n])):
+                    top = cross.astype(BF16)
+                    high[4 * i + n, part, k : k + step, :] = top
+                    low[4 * i + n, part, k : k + step, :] = (cross - top.astype(F32)).astype(BF16)
         return 0
 
-    lax.fori_loop(0, OFFS, pair, 0)
+    lax.fori_loop(0, OFFS // 4, pairs, 0)
     mask, bins = band_masks(edges)
     scale = 1.0 / jnp.sqrt(FRAMES * bins)
     bands = mask.astype(BF16)
+    weights = jnp.concatenate([bands, bands], axis=1)
     for p in range(OFFS):
-        for part in range(2):
-            total = jnp.dot(bands, high[p, part], preferred_element_type=F32)
-            total += jnp.dot(bands, low[p, part], preferred_element_type=F32)
-            out[p, part * BANDS : (part + 1) * BANDS, :] = total * scale
+        real = jnp.concatenate([high[p, 0], low[p, 0]], axis=0)
+        imag = jnp.concatenate([high[p, 1], low[p, 1]], axis=0)
+        total = jnp.dot(
+            weights, jnp.concatenate([real, imag], axis=1), preferred_element_type=F32
+        )
+        out[p, :BANDS, :] = total[:, :WIDTH] * scale
+        out[p, BANDS:, :] = total[:, WIDTH:] * scale
 
 
 def coherences(offsets, edges, own, near, far):
@@ -207,7 +255,6 @@
         out_specs=VMEM,
         scratch_shapes=[
             pltpu.VMEM((3, FRAMES, NFFT, WIDTH), BF16),
-            pltpu.VMEM((FRAMES, NFFT, WIDTH), F32),
             pltpu.VMEM((OFFS, 2, NBIN, WIDTH), BF16),
             pltpu.VMEM((OFFS, 2, NBIN, WIDTH), BF16),
         ],
@@ -284,23 +331,21 @@
     return lax.ppermute(block, axis, route)
 
 
-def groups_of(size, inner):
-    if inner:
-        return [list(range(g * inner, (g + 1) * inner)) for g in range(size // inner)]
-    return [list(range(g, size, 16)) for g in range(16)]
-
-
-def spread_sources(picked):
+def spread_sources(picked, work):
     size = lax.axis_size("ch")
-    runs = groups_of(size, 16)
-    places = groups_of(size, 0)
-    mine = lax.all_to_all(picked, "ch", 0, 0, axis_index_groups=runs, tiled=True)
+    runs = [list(range(g, g + RUN)) for g in range(0, size, RUN)]
+    places = [list(range(g, size, RUN)) for g in range(RUN)]
+    shape = picked.shape
+    mine = picked.reshape(RUN, -1, WIDTH)
+    mine = lax.all_to_all(mine, "ch", 0, 0, axis_index_groups=runs, tiled=True)
     mine = jnp.sum(mine.astype(F32), axis=0).astype(BF16)
-    copies = jnp.broadcast_to(mine[None], (len(places[0]),) + mine.shape)
+    copies = jnp.broadcast_to(mine[None], (size // RUN,) + mine.shape)
     mine = lax.all_to_all(copies, "ch", 0, 0, axis_index_groups=places, tiled=True)
     mine = jnp.sum(mine.astype(F32), axis=0).astype(BF16)
-    copies = jnp.broadcast_to(mine[None], (len(runs[0]),) + mine.shape)
-    return lax.all_to_all(copies, "ch", 0, 0, axis_index_groups=runs, tiled=True)
+    mine, done = lax.optimization_barrier((mine, work()))
+    copies = jnp.broadcast_to(mine[None], (RUN,) + mine.shape)
+    found = lax.all_to_all(copies, "ch", 0, 0, axis_index_groups=runs, tiled=True)
+    return done, found.reshape(shape)
 
 
 def per_device(raw, taps, offsets, sources, edges):
@@ -308,8 +353,9 @@
     white, picked = whiten(raw, taps, edges, sources, first)
     near = from_behind(white, "ch", -1)
     far = from_behind(white, "ch", -2)
+    (near, far), found = spread_sources(picked, lambda: (near, far))
     coherence = coherences(offsets, edges, white, near, far)
-    correlation = correlations(spread_sources(picked), white)
+    correlation = correlations(found, white)
     return (coherence, correlation)
 
 

time: 75.1 us -> 67.3 us (0.90)
  the two profiles are of different devices: /device:TPU:31 before, /device:TPU:1 now
where the time goes in v3:
time: 67.3 us; the launch traced here: 66.6 us
  starting transfers between devices  34.3 us (51%)
  blocking collectives  16 us (24%)
  Pallas kernels  14.6 us (22%)
  between operations  0.75 us (1%)
  local copies, waits for them, and re-layouts  0.72 us (1%)
    all_to_all x1, blocking collectives, spread_sources(): lax.all_to_all(copies, 'ch', 0, 0, axis_index_groups=places, tiled=True)  16 us
    ppermute x2, starting transfers between devices, from_behind(): return lax.ppermute(block, axis, route)  15 us
    all_to_all x1, starting transfers between devices, spread_sources(): mine = lax.all_to_all(mine, 'ch', 0, 0, axis_index_groups=runs, tiled=True)  10.3 us
    all_to_all x1, starting transfers between devices, spread_sources(): lax.all_to_all(copies, 'ch', 0, 0, axis_index_groups=runs, tiled=True)  8.97 us
    pallas_call x1, Pallas kernels, coherences(): pl.pallas_call(coherence_kernel, out_shape=jax.ShapeDtypeStruct((OFFS, 2...  5.96 us
    pallas_call x1, Pallas kernels, whiten(): pl.pallas_call(whiten_kernel, out_shape=(jax.ShapeDtypeStruct((FRAMES, NF...  4.69 us
    pallas_call x1, Pallas kernels, correlations(): pl.pallas_call(correlate_kernel, grid=(SOURCES // S_STEP,), out_shape=jax...  3.97 us
  transfers between devices with their start and end apart: 4, of which 1 were waited for; matrix products, arithmetic and copies ran while one was open for 0% of the time, Pallas kernels for 9%

profile of v3, /device:TPU:1, one launch (start us, length us, event | category | flops | bytes accessed | tf_op | source)
XLA Modules:
  0.0 66.6 jit_solution(4932576507587156633)
XLA Ops:
  0.6 0.0 copy-start.2
  0.6 0.0 copy-start.3
  0.7 4.7 %whiten.1 = (bf16[8,256,128]{2,1,0:T(8,128)(2,1)}, bf16[16,32,128]{2,1,0:T(8,128)(2,1)}) custom-call(s32[1]{0:T(128)} %bitcast.first, f32[16]{0:T(128)} %taps_hbm.1, s32[17]{0:T(128)} %edges.1, s32[32]{0:T(128)} %sources_hbm.1, f32[2,128,640]{2,1,0:T(8,128)} %constant.16.clone.turns_hbm, f32[256,16]{1,0:T(8,128)} %constant.17.clone.tap_turns_hbm, ...), custom_call_target="tpu_custom_call" | custom-call | tf_op jit(solution)/shard_map/whiten/pallas_call | solution.py:173
  5.4 0.0 copy-start
  5.4 0.0 copy-start.1
  5.4 10.3 %all-to-all-start = ((bf16[16,32,128]{2,1,0:T(8,128)(2,1)}), bf16[16,32,128]{2,1,0:T(8,128)(2,1)S(1)}, u32[]{:S(2)}, u32[]{:S(2)}) async-start(bf16[16,32,128]{2,1,0:T(8,128)(2,1)} %get-tuple-element.8), calls=%async_computation | async-start | bytes 262144 | tf_op jit(solution)/shard_map/all_to_all | solution.py:340
  15.7 12.4 %collective-permute-start.1 = (bf16[8,256,128]{2,1,0:T(8,128)(2,1)}, bf16[8,256,128]{2,1,0:T(8,128)(2,1)S(1)}, u32[]{:S(2)}, u32[]{:S(2)}) collective-permute-start(bf16[8,256,128]{2,1,0:T(8,128)(2,1)} %get-tuple-element.7.own.white), channel_id=1, source_target_pairs={{2,0},{3,1},{4,2},{5,3},{6,4},{7,5},{8,6},{9,7},{10,8},{11,9},{12,... | collective-permute-start | bytes 1572872 | tf_op jit(solution)/shard_map/ppermute | solution.py:331
  28.1 2.5 %collective-permute-start = (bf16[8,256,128]{2,1,0:T(8,128)(2,1)}, bf16[8,256,128]{2,1,0:T(8,128)(2,1)S(1)}, u32[]{:S(2)}, u32[]{:S(2)}) collective-permute-start(bf16[8,256,128]{2,1,0:T(8,128)(2,1)} %get-tuple-element.7.own.white), channel_id=1, source_target_pairs={{1,0},{2,1},{3,2},{4,3},{5,4},{6,5},{7,6},{8,7},{9,8},{10,9},{11,1... | collective-permute-start | bytes 1572872 | tf_op jit(solution)/shard_map/ppermute | solution.py:331
  30.7 0.0 all-to-all-done
  30.8 16.0 %all_to_all.15 = bf16[32,32,128]{2,1,0:T(8,128)(2,1)S(1)} all-to-all(bf16[32,32,128]{2,1,0:T(8,128)(2,1)S(1)} %broadcast_in_dim.7), channel_id=1, replica_groups={{0,16,32,48,64,80,96,112,128,144,160,176,192,208,224,240,256,272,288,30..., dimensions={0} | all-to-all | bytes 524288 | tf_op jit(solution)/shard_map/all_to_all | solution.py:343
  46.8 0.1 reduce_sum.25
  46.8 0.0 collective-permute-done.1.far
  46.8 0.0 collective-permute-done.near
  46.9 0.7 broadcast_in_dim.8
  47.5 9.0 %all-to-all-start.2 = ((bf16[16,32,128]{2,1,0:T(8,128)(2,1)}), bf16[16,32,128]{2,1,0:T(8,128)(2,1)S(1)}, u32[]{:S(2)}, u32[]{:S(2)}) async-start(bf16[16,32,128]{2,1,0:T(8,128)(2,1)} %broadcast_in_dim.8), calls=%async_computation.2 | async-start | bytes 262144 | tf_op jit(solution)/shard_map/all_to_all | solution.py:347
  56.5 0.0 copy-done.2
  56.5 0.0 copy-done.3
  56.5 0.0 copy-done
  56.5 6.0 %coherence.1 = f32[16,32,128]{2,1,0:T(8,128)} custom-call(s32[16]{0:T(128)S(1)} %copy-done.3, s32[17]{0:T(128)S(1)} %copy-done.2, bf16[8,256,128]{2,1,0:T(8,128)(2,1)S(1)} %copy-done, bf16[8,256,128]{2,1,0:T(8,128)(2,1)S(1)} %collective-permute-done.near, bf16[8,256,128]{2,1,0:T(8,128)(2,1)S(1)} %collective-permute-done.1.far), custom_call_target="tpu_custom_call" | custom-call | tf_op jit(solution)/shard_map/coherence/pallas_call | solution.py:251
  62.5 0.2 all-to-all-done.2.sources
  62.6 0.0 copy-done.1
  62.6 4.0 %correlate.1 = f32[129,32,128]{2,1,0:T(8,128)} custom-call(bf16[288,256]{1,0:T(8,128)(2,1)S(1)} %copy-done.1, bf16[16,32,128]{2,1,0:T(8,128)(2,1)S(1)} %all-to-all-done.2.sources, bf16[8,256,128]{2,1,0:T(8,128)(2,1)S(1)} %copy-done), custom_call_target="tpu_custom_call" | custom-call | tf_op jit(solution)/shard_map/correlate/pallas_call | solution.py:308
  (2 shorter events, 0.1 us)
Async XLA Ops:
  0.6 55.9 %copy-start.2 = (s32[17]{0:T(128)S(1)}, s32[17]{0:T(128)}, u32[]{:S(2)}) copy-start(s32[17]{0:T(128)} %edges.1) | copy-start | bytes 208
  0.6 55.8 %copy-start.3 = (s32[16]{0:T(128)S(1)}, s32[16]{0:T(128)}, u32[]{:S(2)}) copy-start(s32[16]{0:T(128)} %offsets.1) | copy-start | bytes 196
  5.4 51.1 %copy-start = (bf16[8,256,128]{2,1,0:T(8,128)(2,1)S(1)}, bf16[8,256,128]{2,1,0:T(8,128)(2,1)}, u32[]{:S(2)}) copy-start(bf16[8,256,128]{2,1,0:T(8,128)(2,1)} %get-tuple-element.7.own.white) | copy-start | bytes 1572868
  5.4 57.3 %copy-start.1 = (bf16[288,256]{1,0:T(8,128)(2,1)S(1)}, bf16[288,256]{1,0:T(8,128)(2,1)}, u32[]{:S(2)}) copy-start(bf16[288,256]{1,0:T(8,128)(2,1)} %constant.18.clone.table) | copy-start | bytes 442372
  5.4 25.3 %all-to-all-start = ((bf16[16,32,128]{2,1,0:T(8,128)(2,1)}), bf16[16,32,128]{2,1,0:T(8,128)(2,1)S(1)}, u32[]{:S(2)}, u32[]{:S(2)}) async-start(bf16[16,32,128]{2,1,0:T(8,128)(2,1)} %get-tuple-element.8), calls=%async_computation | async-start | bytes 262144 | tf_op jit(solution)/shard_map/all_to_all | solution.py:340
  15.7 31.1 %collective-permute-start.1 = (bf16[8,256,128]{2,1,0:T(8,128)(2,1)}, bf16[8,256,128]{2,1,0:T(8,128)(2,1)S(1)}, u32[]{:S(2)}, u32[]{:S(2)}) collective-permute-start(bf16[8,256,128]{2,1,0:T(8,128)(2,1)} %get-tuple-element.7.own.white), channel_id=1, source_target_pairs={{2,0},{3,1},{4,2},{5,3},{6,4},{7,5},{8,6},{9,7},{10,8},{11,9},{12,... | collective-permute-start | bytes 1572872 | tf_op jit(solution)/shard_map/ppermute | solution.py:331
  28.1 18.7 %collective-permute-start = (bf16[8,256,128]{2,1,0:T(8,128)(2,1)}, bf16[8,256,128]{2,1,0:T(8,128)(2,1)S(1)}, u32[]{:S(2)}, u32[]{:S(2)}) collective-permute-start(bf16[8,256,128]{2,1,0:T(8,128)(2,1)} %get-tuple-element.7.own.white), channel_id=1, source_target_pairs={{1,0},{2,1},{3,2},{4,3},{5,4},{6,5},{7,6},{8,7},{9,8},{10,9},{11,1... | collective-permute-start | bytes 1572872 | tf_op jit(solution)/shard_map/ppermute | solution.py:331
  47.5 15.1 %all-to-all-start.2 = ((bf16[16,32,128]{2,1,0:T(8,128)(2,1)}), bf16[16,32,128]{2,1,0:T(8,128)(2,1)S(1)}, u32[]{:S(2)}, u32[]{:S(2)}) async-start(bf16[16,32,128]{2,1,0:T(8,128)(2,1)} %broadcast_in_dim.8), calls=%async_computation.2 | async-start | bytes 262144 | tf_op jit(solution)/shard_map/all_to_all | solution.py:347

commit v4 on v3

--- a/solution.py
+++ b/solution.py
@@ -266,9 +266,8 @@
 S_STEP = 8
 
 
-def correlate_kernel(table, sources, white, out, left, high, low):
-    @pl.when(pl.program_id(0) == 0)
-    def _():
+def correlate_kernel(table, sources, white, out, left, high, low, held, sems):
+    if True:
         row = lax.broadcasted_iota(jnp.int32, (CHUNK, NFFT), 0)
         column = lax.broadcasted_iota(jnp.int32, (CHUNK, NFFT), 1)
         diagonal = (column % CHUNK) == row
@@ -293,32 +292,39 @@
                     start = part * NBIN + c * CHUNK
                     kept[:, start : start + CHUNK, :] = value[:, :, part * WIDTH : (part + 1) * WIDTH]
 
-    base = pl.program_id(0) * S_STEP
-    for i in range(0, S_STEP, 2):
-        top = jnp.concatenate([high[base + i], high[base + i + 1]], axis=1)
-        rest = jnp.concatenate([low[base + i], low[base + i + 1]], axis=1)
-        both = jnp.dot(table[...], top, preferred_element_type=F32)
-        lagged = both[:LAG_ROWS] + both[LAG_ROWS:]
-        lagged += jnp.dot(table[:LAG_ROWS, :], rest, preferred_element_type=F32)
-        out[:, i, :] = lagged[:LAGS, :WIDTH]
-        out[:, i + 1, :] = lagged[:LAGS, WIDTH:]
+    copies = []
+    for g in range(SOURCES // S_STEP):
+        for i in range(0, S_STEP, 2):
+            s = g * S_STEP + i
+            top = jnp.concatenate([high[s], high[s + 1]], axis=1)
+            rest = jnp.concatenate([low[s], low[s + 1]], axis=1)
+            both = jnp.dot(table[...], top, preferred_element_type=F32)
+            lagged = both[:LAG_ROWS] + both[LAG_ROWS:]
+            lagged += jnp.dot(table[:LAG_ROWS, :], rest, preferred_element_type=F32)
+            held[g, :, i, :] = lagged[:LAGS, :WIDTH]
+            held[g, :, i + 1, :] = lagged[:LAGS, WIDTH:]
+        copies.append(
+            pltpu.make_async_copy(
+                held.at[g], out.at[:, pl.ds(g * S_STEP, S_STEP), :], sems.at[g]
+            )
+        )
+        copies[-1].start()
+    for copy in copies:
+        copy.wait()
 
 
 def correlations(sources, white):
     return pl.pallas_call(
         correlate_kernel,
-        grid=(SOURCES // S_STEP,),
         out_shape=jax.ShapeDtypeStruct((LAGS, SOURCES, WIDTH), F32),
-        in_specs=[
-            pl.BlockSpec((2 * LAG_ROWS, NFFT), lambda g: (0, 0)),
-            pl.BlockSpec((2 * CHUNKS, SOURCES, WIDTH), lambda g: (0, 0, 0)),
-            pl.BlockSpec((FRAMES, NFFT, WIDTH), lambda g: (0, 0, 0)),
-        ],
-        out_specs=pl.BlockSpec((LAGS, S_STEP, WIDTH), lambda g: (0, g, 0)),
+        in_specs=[VMEM] * 3,
+        out_specs=pl.BlockSpec(memory_space=pl.ANY),
         scratch_shapes=[
             pltpu.VMEM((SOURCES * CHUNK, NFFT), BF16),
             pltpu.VMEM((SOURCES, NFFT, WIDTH), BF16),
             pltpu.VMEM((SOURCES, NFFT, WIDTH), BF16),
+            pltpu.VMEM((SOURCES // S_STEP, LAGS, S_STEP, WIDTH), F32),
+            pltpu.SemaphoreType.DMA((SOURCES // S_STEP,)),
         ],
         compiler_params=pltpu.CompilerParams(vmem_limit_bytes=VMEM_LIMIT),
         name="correlate",
@@ -329,6 +335,23 @@
     devices = range(lax.axis_size(axis))
     route = [((i - distance) % len(devices), i) for i in devices]
     return lax.ppermute(block, axis, route)
+
+
+def sum_kernel(parts, out):
+    total = jnp.sum(parts[...].astype(F32), axis=0).astype(BF16)
+    out[...] = jnp.broadcast_to(total[None], out.shape)
+
+
+def sum_copies(parts, count):
+    return pl.pallas_call(
+        sum_kernel,
+        out_shape=jax.ShapeDtypeStruct((count,) + parts.shape[1:], BF16),
+        in_specs=[VMEM],
+        out_specs=VMEM,
+        cost_estimate=pl.CostEstimate(flops=10_000, bytes_accessed=1 << 20, transcendentals=0),
+        compiler_params=pltpu.CompilerParams(vmem_limit_bytes=VMEM_LIMIT),
+        name="sum_copies",
+    )(parts)
 
 
 def spread_sources(picked, work):
@@ -338,12 +361,10 @@
     shape = picked.shape
     mine = picked.reshape(RUN, -1, WIDTH)
     mine = lax.all_to_all(mine, "ch", 0, 0, axis_index_groups=runs, tiled=True)
-    mine = jnp.sum(mine.astype(F32), axis=0).astype(BF16)
-    copies = jnp.broadcast_to(mine[None], (size // RUN,) + mine.shape)
+    copies = sum_copies(mine, size // RUN)
     mine = lax.all_to_all(copies, "ch", 0, 0, axis_index_groups=places, tiled=True)
-    mine = jnp.sum(mine.astype(F32), axis=0).astype(BF16)
-    mine, done = lax.optimization_barrier((mine, work()))
-    copies = jnp.broadcast_to(mine[None], (RUN,) + mine.shape)
+    copies = sum_copies(mine, RUN)
+    copies, done = lax.optimization_barrier((copies, work()))
     found = lax.all_to_all(copies, "ch", 0, 0, axis_index_groups=runs, tiled=True)
     return done, found.reshape(shape)
 

time: 67.3 us -> 66.2 us (0.984)
  local copies, waits for them, and re-layouts: 0.72 us -> 0.02 us
    broadcast_in_dim x2 -> x0, local copies, waits for them, and re-layouts: 0.7 us -> none  [the longest x1 0.66 us: spread_sources(): copies = jnp.broadcast_to(mine[None], (RUN,) + mine.shape)]
    pallas_call x1 -> x3, Pallas kernels: 3.97 us -> 3.72 us  [the longest x1 2.99 us: correlations(): pl.pallas_call(correlate_kernel, out_shape=jax.ShapeDtypeStruct((LAGS, SO...]
  transfers between devices with their start and end apart: 4 -> 4, of which waited for: 1 -> 1; matrix products, arithmetic and copies ran while one was open for 0% -> 0% of each run, Pallas kernels for 9% -> 10%
where the time goes in v4:
time: 66.2 us; the launch traced here: 65.6 us
  starting transfers between devices  34.3 us (52%)
  blocking collectives  16 us (24%)
  Pallas kernels  14.4 us (22%)
  between operations  0.73 us (1%)
    all_to_all x1, blocking collectives, spread_sources(): lax.all_to_all(copies, 'ch', 0, 0, axis_index_groups=places, tiled=True)  16 us
    ppermute x2, starting transfers between devices, from_behind(): return lax.ppermute(block, axis, route)  15 us
    all_to_all x1, starting transfers between devices, spread_sources(): mine = lax.all_to_all(mine, 'ch', 0, 0, axis_index_groups=runs, tiled=True)  10.3 us
    all_to_all x1, starting transfers between devices, spread_sources(): lax.all_to_all(copies, 'ch', 0, 0, axis_index_groups=runs, tiled=True)  9.01 us
    pallas_call x1, Pallas kernels, coherences(): pl.pallas_call(coherence_kernel, out_shape=jax.ShapeDtypeStruct((OFFS, 2...  5.96 us
    pallas_call x1, Pallas kernels, whiten(): pl.pallas_call(whiten_kernel, out_shape=(jax.ShapeDtypeStruct((FRAMES, NF...  4.69 us
    pallas_call x1, Pallas kernels, correlations(): pl.pallas_call(correlate_kernel, out_shape=jax.ShapeDtypeStruct((LAGS, SO...  2.99 us
  transfers between devices with their start and end apart: 4, of which 1 were waited for; matrix products, arithmetic and copies ran while one was open for 0% of the time, Pallas kernels for 10%

profile of v4, /device:TPU:1, one launch (start us, length us, event | category | flops | bytes accessed | tf_op | source)
XLA Modules:
  0.0 65.6 jit_solution(7816238158606178223)
XLA Ops:
  0.6 0.0 copy-start.2
  0.6 0.0 copy-start.3
  0.7 4.7 %whiten.1 = (bf16[8,256,128]{2,1,0:T(8,128)(2,1)}, bf16[16,32,128]{2,1,0:T(8,128)(2,1)}) custom-call(s32[1]{0:T(128)} %bitcast.first, f32[16]{0:T(128)} %taps_hbm.1, s32[17]{0:T(128)} %edges.1, s32[32]{0:T(128)} %sources_hbm.1, f32[2,128,640]{2,1,0:T(8,128)} %constant.12.clone.turns_hbm, f32[256,16]{1,0:T(8,128)} %constant.13.clone.tap_turns_hbm, ...), custom_call_target="tpu_custom_call" | custom-call | tf_op jit(solution)/shard_map/whiten/pallas_call | solution.py:173
  5.4 0.0 copy-start
  5.4 0.0 copy-start.1
  5.4 10.3 %all-to-all-start = ((bf16[16,32,128]{2,1,0:T(8,128)(2,1)}), bf16[16,32,128]{2,1,0:T(8,128)(2,1)S(1)}, u32[]{:S(2)}, u32[]{:S(2)}) async-start(bf16[16,32,128]{2,1,0:T(8,128)(2,1)} %get-tuple-element.8), calls=%async_computation | async-start | bytes 262144 | tf_op jit(solution)/shard_map/all_to_all | solution.py:363
  15.7 12.4 %collective-permute-start.1 = (bf16[8,256,128]{2,1,0:T(8,128)(2,1)}, bf16[8,256,128]{2,1,0:T(8,128)(2,1)S(1)}, u32[]{:S(2)}, u32[]{:S(2)}) collective-permute-start(bf16[8,256,128]{2,1,0:T(8,128)(2,1)} %get-tuple-element.7.own.white), channel_id=1, source_target_pairs={{2,0},{3,1},{4,2},{5,3},{6,4},{7,5},{8,6},{9,7},{10,8},{11,9},{12,... | collective-permute-start | bytes 1572872 | tf_op jit(solution)/shard_map/ppermute | solution.py:337
  28.1 2.5 %collective-permute-start = (bf16[8,256,128]{2,1,0:T(8,128)(2,1)}, bf16[8,256,128]{2,1,0:T(8,128)(2,1)S(1)}, u32[]{:S(2)}, u32[]{:S(2)}) collective-permute-start(bf16[8,256,128]{2,1,0:T(8,128)(2,1)} %get-tuple-element.7.own.white), channel_id=1, source_target_pairs={{1,0},{2,1},{3,2},{4,3},{5,4},{6,5},{7,6},{8,7},{9,8},{10,9},{11,1... | collective-permute-start | bytes 1572872 | tf_op jit(solution)/shard_map/ppermute | solution.py:337
  30.7 0.0 all-to-all-done.parts
  30.7 16.0 %all_to_all.15.parts = bf16[32,32,128]{2,1,0:T(8,128)(2,1)S(1)} all-to-all(bf16[32,32,128]{2,1,0:T(8,128)(2,1)S(1)} %sum_copies.2), channel_id=1, replica_groups={{0,16,32,48,64,80,96,112,128,144,160,176,192,208,224,240,256,272,288,30..., dimensions={0} | all-to-all | bytes 524288 | tf_op jit(solution)/shard_map/all_to_all | solution.py:365
  46.7 0.7 %sum_copies.3 = bf16[16,32,128]{2,1,0:T(8,128)(2,1)} custom-call(bf16[32,32,128]{2,1,0:T(8,128)(2,1)S(1)} %all_to_all.15.parts), custom_call_target="tpu_custom_call" | custom-call | flops 10000 | bytes 1048576 | tf_op jit(solution)/shard_map/sum_copies/pallas_call | solution.py:346
  47.4 0.0 collective-permute-done.1.far
  47.4 0.0 collective-permute-done.near
  47.4 9.0 %all-to-all-start.2 = ((bf16[16,32,128]{2,1,0:T(8,128)(2,1)}), bf16[16,32,128]{2,1,0:T(8,128)(2,1)S(1)}, u32[]{:S(2)}, u32[]{:S(2)}) async-start(bf16[16,32,128]{2,1,0:T(8,128)(2,1)} %sum_copies.3), calls=%async_computation.2 | async-start | bytes 262144 | tf_op jit(solution)/shard_map/all_to_all | solution.py:368
  56.5 0.0 copy-done.2
  56.5 0.0 copy-done.3
  56.5 0.0 copy-done
  56.5 6.0 %coherence.1 = f32[16,32,128]{2,1,0:T(8,128)} custom-call(s32[16]{0:T(128)S(1)} %copy-done.3, s32[17]{0:T(128)S(1)} %copy-done.2, bf16[8,256,128]{2,1,0:T(8,128)(2,1)S(1)} %copy-done, bf16[8,256,128]{2,1,0:T(8,128)(2,1)S(1)} %collective-permute-done.near, bf16[8,256,128]{2,1,0:T(8,128)(2,1)S(1)} %collective-permute-done.1.far), custom_call_target="tpu_custom_call" | custom-call | tf_op jit(solution)/shard_map/coherence/pallas_call | solution.py:251
  62.4 0.2 all-to-all-done.2.sources
  62.6 0.0 copy-done.1
  62.6 3.0 %correlate.1 = f32[129,32,128]{2,1,0:T(8,128)} custom-call(bf16[288,256]{1,0:T(8,128)(2,1)S(1)} %copy-done.1, bf16[16,32,128]{2,1,0:T(8,128)(2,1)S(1)} %all-to-all-done.2.sources, bf16[8,256,128]{2,1,0:T(8,128)(2,1)S(1)} %copy-done), custom_call_target="tpu_custom_call" | custom-call | tf_op jit(solution)/shard_map/correlate/pallas_call | solution.py:317
  (1 shorter events, 0.0 us)
Async XLA Ops:
  0.6 55.8 %copy-start.2 = (s32[17]{0:T(128)S(1)}, s32[17]{0:T(128)}, u32[]{:S(2)}) copy-start(s32[17]{0:T(128)} %edges.1) | copy-start | bytes 208
  0.6 55.8 %copy-start.3 = (s32[16]{0:T(128)S(1)}, s32[16]{0:T(128)}, u32[]{:S(2)}) copy-start(s32[16]{0:T(128)} %offsets.1) | copy-start | bytes 196
  5.4 51.1 %copy-start = (bf16[8,256,128]{2,1,0:T(8,128)(2,1)S(1)}, bf16[8,256,128]{2,1,0:T(8,128)(2,1)}, u32[]{:S(2)}) copy-start(bf16[8,256,128]{2,1,0:T(8,128)(2,1)} %get-tuple-element.7.own.white) | copy-start | bytes 1572868
  5.4 57.2 %copy-start.1 = (bf16[288,256]{1,0:T(8,128)(2,1)S(1)}, bf16[288,256]{1,0:T(8,128)(2,1)}, u32[]{:S(2)}) copy-start(bf16[288,256]{1,0:T(8,128)(2,1)} %constant.14.clone.table) | copy-start | bytes 442372
  5.4 25.3 %all-to-all-start = ((bf16[16,32,128]{2,1,0:T(8,128)(2,1)}), bf16[16,32,128]{2,1,0:T(8,128)(2,1)S(1)}, u32[]{:S(2)}, u32[]{:S(2)}) async-start(bf16[16,32,128]{2,1,0:T(8,128)(2,1)} %get-tuple-element.8), calls=%async_computation | async-start | bytes 262144 | tf_op jit(solution)/shard_map/all_to_all | solution.py:363
  15.7 31.7 %collective-permute-start.1 = (bf16[8,256,128]{2,1,0:T(8,128)(2,1)}, bf16[8,256,128]{2,1,0:T(8,128)(2,1)S(1)}, u32[]{:S(2)}, u32[]{:S(2)}) collective-permute-start(bf16[8,256,128]{2,1,0:T(8,128)(2,1)} %get-tuple-element.7.own.white), channel_id=1, source_target_pairs={{2,0},{3,1},{4,2},{5,3},{6,4},{7,5},{8,6},{9,7},{10,8},{11,9},{12,... | collective-permute-start | bytes 1572872 | tf_op jit(solution)/shard_map/ppermute | solution.py:337
  28.1 19.3 %collective-permute-start = (bf16[8,256,128]{2,1,0:T(8,128)(2,1)}, bf16[8,256,128]{2,1,0:T(8,128)(2,1)S(1)}, u32[]{:S(2)}, u32[]{:S(2)}) collective-permute-start(bf16[8,256,128]{2,1,0:T(8,128)(2,1)} %get-tuple-element.7.own.white), channel_id=1, source_target_pairs={{1,0},{2,1},{3,2},{4,3},{5,4},{6,5},{7,6},{8,7},{9,8},{10,9},{11,1... | collective-permute-start | bytes 1572872 | tf_op jit(solution)/shard_map/ppermute | solution.py:337
  47.4 15.2 %all-to-all-start.2 = ((bf16[16,32,128]{2,1,0:T(8,128)(2,1)}), bf16[16,32,128]{2,1,0:T(8,128)(2,1)S(1)}, u32[]{:S(2)}, u32[]{:S(2)}) async-start(bf16[16,32,128]{2,1,0:T(8,128)(2,1)} %sum_copies.3), calls=%async_computation.2 | async-start | bytes 262144 | tf_op jit(solution)/shard_map/all_to_all | solution.py:368

commit v5 on v4

--- a/solution.py
+++ b/solution.py
@@ -193,11 +193,19 @@
     )(first, taps, edges, sources, jnp.asarray(turns), jnp.asarray(tap_turns), raw)
 
 
-def coherence_kernel(offsets, edges, own, near, far, out, ext, high, low):
+def coherence_kernel(odd, offsets, edges, own, other, arrived, swapped, out, ext, high, low):
     for f in range(FRAMES):
         ext[0, f] = own[f]
-        ext[1, f] = near[f]
-        ext[2, f] = far[f]
+        ext[2, f] = swapped[f]
+
+    @pl.when(odd[0] == 0)
+    def _():
+        ext[1] = other[...]
+
+    @pl.when(odd[0] == 1)
+    def _():
+        ext[1] = arrived[...]
+
     lane = lax.broadcasted_iota(jnp.int32, (1, WIDTH), 1)
     step = 16
 
@@ -247,11 +255,11 @@
         out[p, BANDS:, :] = total[:, WIDTH:] * scale
 
 
-def coherences(offsets, edges, own, near, far):
+def coherences(odd, offsets, edges, own, other, arrived, swapped):
     return pl.pallas_call(
         coherence_kernel,
         out_shape=jax.ShapeDtypeStruct((OFFS, 2 * BANDS, WIDTH), F32),
-        in_specs=[SMEM] * 2 + [VMEM] * 3,
+        in_specs=[SMEM] * 3 + [VMEM] * 4,
         out_specs=VMEM,
         scratch_shapes=[
             pltpu.VMEM((3, FRAMES, NFFT, WIDTH), BF16),
@@ -260,7 +268,7 @@
         ],
         compiler_params=pltpu.CompilerParams(vmem_limit_bytes=VMEM_LIMIT),
         name="coherence",
-    )(offsets, edges, own, near, far)
+    )(odd, offsets, edges, own, other, arrived, swapped)
 
 
 S_STEP = 8
@@ -331,10 +339,14 @@
     )(jnp.asarray(lag_tables()), sources, white).transpose(1, 0, 2)
 
 
-def from_behind(block, axis, distance):
-    devices = range(lax.axis_size(axis))
-    route = [((i - distance) % len(devices), i) for i in devices]
-    return lax.ppermute(block, axis, route)
+def from_next_chip(block):
+    size = lax.axis_size("ch")
+    route = [((i + 3 if i % 2 == 0 else i + 1) % size, i) for i in range(size)]
+    return lax.ppermute(block, "ch", route)
+
+
+def swap_in_chip(block):
+    return lax.ppermute(block, "ch", [(i ^ 1, i) for i in range(lax.axis_size("ch"))])
 
 
 def sum_kernel(parts, out):
@@ -372,10 +384,13 @@
 def per_device(raw, taps, offsets, sources, edges):
     first = jnp.full((1,), lax.axis_index("ch") * WIDTH, jnp.int32)
     white, picked = whiten(raw, taps, edges, sources, first)
-    near = from_behind(white, "ch", -1)
-    far = from_behind(white, "ch", -2)
-    (near, far), found = spread_sources(picked, lambda: (near, far))
-    coherence = coherences(offsets, edges, white, near, far)
+    odd = jnp.full((1,), lax.axis_index("ch") % 2, jnp.int32)
+    arrived = from_next_chip(white)
+    other = swap_in_chip(white)
+    held, found = spread_sources(picked, lambda: (other, arrived))
+    other, arrived = held
+    coherence = coherences(odd, offsets, edges, white, other, arrived, swap_in_chip(arrived))
+    coherence, found = lax.optimization_barrier((coherence, found))
     correlation = correlations(found, white)
     return (coherence, correlation)
 

time: 66.2 us -> 65 us (0.982)
  starting transfers between devices: 34.3 us -> 32.7 us
  blocking collectives: 16 us -> 16.7 us
    all_to_all x1, starting transfers between devices: 9.01 us -> 3.42 us  [spread_sources(): lax.all_to_all(copies, 'ch', 0, 0, axis_index_groups=runs, tiled=True)]
    ppermute x2 -> x3, starting transfers between devices: 15 us -> 18.9 us  [the longest x1 12.7 us: from_next_chip(): return lax.ppermute(block, 'ch', route)]
    all_to_all x1, blocking collectives: 16 us -> 16.7 us  [spread_sources(): lax.all_to_all(copies, 'ch', 0, 0, axis_index_groups=places, tiled=True)]
  transfers between devices with their start and end apart: 4 -> 5, of which waited for: 1 -> 1; matrix products, arithmetic and copies ran while one was open for 0% -> 0% of each run, Pallas kernels for 10% -> 10%
where the time goes in v5:
time: 65 us; the launch traced here: 64.6 us
  starting transfers between devices  32.7 us (50%)
  blocking collectives  16.7 us (26%)
  Pallas kernels  14.4 us (22%)
  between operations  0.77 us (1%)
    all_to_all x1, blocking collectives, spread_sources(): lax.all_to_all(copies, 'ch', 0, 0, axis_index_groups=places, tiled=True)  16.7 us
    ppermute x1, starting transfers between devices, from_next_chip(): return lax.ppermute(block, 'ch', route)  12.7 us
    all_to_all x1, starting transfers between devices, spread_sources(): mine = lax.all_to_all(mine, 'ch', 0, 0, axis_index_groups=runs, tiled=True)  10.3 us
    ppermute x2, starting transfers between devices, swap_in_chip(): lax.ppermute(block, 'ch', [(i ^ 1, i) for i in range(lax.axis_size('ch'))])  6.28 us
    pallas_call x1, Pallas kernels, coherences(): pl.pallas_call(coherence_kernel, out_shape=jax.ShapeDtypeStruct((OFFS, 2...  5.97 us
    pallas_call x1, Pallas kernels, whiten(): pl.pallas_call(whiten_kernel, out_shape=(jax.ShapeDtypeStruct((FRAMES, NF...  4.69 us
    all_to_all x1, starting transfers between devices, spread_sources(): lax.all_to_all(copies, 'ch', 0, 0, axis_index_groups=runs, tiled=True)  3.42 us
    pallas_call x1, Pallas kernels, correlations(): pl.pallas_call(correlate_kernel, out_shape=jax.ShapeDtypeStruct((LAGS, SO...  2.99 us
  transfers between devices with their start and end apart: 5, of which 1 were waited for; matrix products, arithmetic and copies ran while one was open for 0% of the time, Pallas kernels for 10%

profile of v5, /device:TPU:1, one launch (start us, length us, event | category | flops | bytes accessed | tf_op | source)
XLA Modules:
  0.0 64.6 jit_solution(13400844224596970072)
XLA Ops:
  0.6 0.0 copy-start.2
  0.6 0.0 copy-start.3
  0.7 4.7 %whiten.1 = (bf16[8,256,128]{2,1,0:T(8,128)(2,1)}, bf16[16,32,128]{2,1,0:T(8,128)(2,1)}) custom-call(s32[1]{0:T(128)} %bitcast.1.first, f32[16]{0:T(128)} %taps_hbm.1, s32[17]{0:T(128)} %edges.1, s32[32]{0:T(128)} %sources_hbm.1, f32[2,128,640]{2,1,0:T(8,128)} %constant.25.clone.turns_hbm, f32[256,16]{1,0:T(8,128)} %constant.26.clone.tap_turns_hbm, ...), custom_call_target="tpu_custom_call" | custom-call | tf_op jit(solution)/shard_map/whiten/pallas_call | solution.py:173
  5.4 0.0 copy-start
  5.4 0.0 copy-start.1
  5.4 10.3 %all-to-all-start = ((bf16[16,32,128]{2,1,0:T(8,128)(2,1)}), bf16[16,32,128]{2,1,0:T(8,128)(2,1)S(1)}, u32[]{:S(2)}, u32[]{:S(2)}) async-start(bf16[16,32,128]{2,1,0:T(8,128)(2,1)} %get-tuple-element.10), calls=%async_computation | async-start | bytes 262144 | tf_op jit(solution)/shard_map/all_to_all | solution.py:375
  15.7 12.7 %collective-permute-start.1 = (bf16[8,256,128]{2,1,0:T(8,128)(2,1)}, bf16[8,256,128]{2,1,0:T(8,128)(2,1)S(1)}, u32[]{:S(2)}, u32[]{:S(2)}) collective-permute-start(bf16[8,256,128]{2,1,0:T(8,128)(2,1)} %get-tuple-element.9.own.white), channel_id=1, source_target_pairs={{3,0},{2,1},{5,2},{4,3},{7,4},{6,5},{9,6},{8,7},{11,8},{10,9},{13,... | collective-permute-start | bytes 1572872 | tf_op jit(solution)/shard_map/ppermute | solution.py:345
  28.4 2.1 %collective-permute-start = (bf16[8,256,128]{2,1,0:T(8,128)(2,1)}, bf16[8,256,128]{2,1,0:T(8,128)(2,1)S(1)}, u32[]{:S(2)}, u32[]{:S(2)}) collective-permute-start(bf16[8,256,128]{2,1,0:T(8,128)(2,1)} %get-tuple-element.9.own.white), channel_id=1, source_target_pairs={{1,0},{0,1},{3,2},{2,3},{5,4},{4,5},{7,6},{6,7},{9,8},{8,9},{11,10... | collective-permute-start | bytes 1572872 | tf_op jit(solution)/shard_map/ppermute | solution.py:349
  30.4 0.0 all-to-all-done.parts
  30.5 16.7 %all_to_all.15.parts = bf16[32,32,128]{2,1,0:T(8,128)(2,1)S(1)} all-to-all(bf16[32,32,128]{2,1,0:T(8,128)(2,1)S(1)} %sum_copies.2), channel_id=1, replica_groups={{0,16,32,48,64,80,96,112,128,144,160,176,192,208,224,240,256,272,288,30..., dimensions={0} | all-to-all | bytes 524288 | tf_op jit(solution)/shard_map/all_to_all | solution.py:377
  47.2 0.7 %sum_copies.3 = bf16[16,32,128]{2,1,0:T(8,128)(2,1)} custom-call(bf16[32,32,128]{2,1,0:T(8,128)(2,1)S(1)} %all_to_all.15.parts), custom_call_target="tpu_custom_call" | custom-call | flops 10000 | bytes 1048576 | tf_op jit(solution)/shard_map/sum_copies/pallas_call | solution.py:358
  47.9 0.0 collective-permute-done.1.arrived
  47.9 0.0 collective-permute-done.other
  47.9 4.2 %collective-permute-start.2 = (bf16[8,256,128]{2,1,0:T(8,128)(2,1)S(1)}, bf16[8,256,128]{2,1,0:T(8,128)(2,1)S(1)}, u32[]{:S(2)}, u32[]{:S(2)}) collective-permute-start(bf16[8,256,128]{2,1,0:T(8,128)(2,1)S(1)} %collective-permute-done.1.arrived), channel_id=1, source_target_pairs={{1,0},{0,1},{3,2},{2,3},{5,4},{4,5},{7,6},{6,7},{9,8},{8,9},{11,10... | collective-permute-start | bytes 1572872 | tf_op jit(solution)/shard_map/ppermute | solution.py:349
  52.1 3.4 %all-to-all-start.2 = ((bf16[16,32,128]{2,1,0:T(8,128)(2,1)}), bf16[16,32,128]{2,1,0:T(8,128)(2,1)S(1)}, u32[]{:S(2)}, u32[]{:S(2)}) async-start(bf16[16,32,128]{2,1,0:T(8,128)(2,1)} %sum_copies.3), calls=%async_computation.2 | async-start | bytes 262144 | tf_op jit(solution)/shard_map/all_to_all | solution.py:380
  55.5 0.0 collective-permute-done.2.swapped
  55.5 0.0 copy-done.2
  55.5 0.0 copy-done.3
  55.6 0.0 copy-done
  55.6 6.0 %coherence.1 = f32[16,32,128]{2,1,0:T(8,128)} custom-call(s32[1]{0:T(128)} %bitcast.odd, s32[16]{0:T(128)S(1)} %copy-done.3, s32[17]{0:T(128)S(1)} %copy-done.2, bf16[8,256,128]{2,1,0:T(8,128)(2,1)S(1)} %copy-done, bf16[8,256,128]{2,1,0:T(8,128)(2,1)S(1)} %collective-permute-done.other, bf16[8,256,128]{2,1,0:T(8,128)(2,1)S(1)} %collective-permute-done.1.arrived, ...), custom_call_target="tpu_custom_call" | custom-call | tf_op jit(solution)/shard_map/coherence/pallas_call | solution.py:259
  61.5 0.1 all-to-all-done.2.sources
  61.6 0.0 copy-done.1
  61.6 3.0 %correlate.1 = f32[129,32,128]{2,1,0:T(8,128)} custom-call(bf16[288,256]{1,0:T(8,128)(2,1)S(1)} %copy-done.1, bf16[16,32,128]{2,1,0:T(8,128)(2,1)S(1)} %all-to-all-done.2.sources, bf16[8,256,128]{2,1,0:T(8,128)(2,1)S(1)} %copy-done), custom_call_target="tpu_custom_call" | custom-call | tf_op jit(solution)/shard_map/correlate/pallas_call | solution.py:325
  (1 shorter events, 0.0 us)
Async XLA Ops:
  0.6 54.9 %copy-start.2 = (s32[17]{0:T(128)S(1)}, s32[17]{0:T(128)}, u32[]{:S(2)}) copy-start(s32[17]{0:T(128)} %edges.1) | copy-start | bytes 208
  0.6 54.9 %copy-start.3 = (s32[16]{0:T(128)S(1)}, s32[16]{0:T(128)}, u32[]{:S(2)}) copy-start(s32[16]{0:T(128)} %offsets.1) | copy-start | bytes 196
  5.4 50.2 %copy-start = (bf16[8,256,128]{2,1,0:T(8,128)(2,1)S(1)}, bf16[8,256,128]{2,1,0:T(8,128)(2,1)}, u32[]{:S(2)}) copy-start(bf16[8,256,128]{2,1,0:T(8,128)(2,1)} %get-tuple-element.9.own.white) | copy-start | bytes 1572868
  5.4 56.3 %copy-start.1 = (bf16[288,256]{1,0:T(8,128)(2,1)S(1)}, bf16[288,256]{1,0:T(8,128)(2,1)}, u32[]{:S(2)}) copy-start(bf16[288,256]{1,0:T(8,128)(2,1)} %constant.27.clone.table) | copy-start | bytes 442372
  5.4 25.1 %all-to-all-start = ((bf16[16,32,128]{2,1,0:T(8,128)(2,1)}), bf16[16,32,128]{2,1,0:T(8,128)(2,1)S(1)}, u32[]{:S(2)}, u32[]{:S(2)}) async-start(bf16[16,32,128]{2,1,0:T(8,128)(2,1)} %get-tuple-element.10), calls=%async_computation | async-start | bytes 262144 | tf_op jit(solution)/shard_map/all_to_all | solution.py:375
  15.7 32.2 %collective-permute-start.1 = (bf16[8,256,128]{2,1,0:T(8,128)(2,1)}, bf16[8,256,128]{2,1,0:T(8,128)(2,1)S(1)}, u32[]{:S(2)}, u32[]{:S(2)}) collective-permute-start(bf16[8,256,128]{2,1,0:T(8,128)(2,1)} %get-tuple-element.9.own.white), channel_id=1, source_target_pairs={{3,0},{2,1},{5,2},{4,3},{7,4},{6,5},{9,6},{8,7},{11,8},{10,9},{13,... | collective-permute-start | bytes 1572872 | tf_op jit(solution)/shard_map/ppermute | solution.py:345
  28.4 19.5 %collective-permute-start = (bf16[8,256,128]{2,1,0:T(8,128)(2,1)}, bf16[8,256,128]{2,1,0:T(8,128)(2,1)S(1)}, u32[]{:S(2)}, u32[]{:S(2)}) collective-permute-start(bf16[8,256,128]{2,1,0:T(8,128)(2,1)} %get-tuple-element.9.own.white), channel_id=1, source_target_pairs={{1,0},{0,1},{3,2},{2,3},{5,4},{4,5},{7,6},{6,7},{9,8},{8,9},{11,10... | collective-permute-start | bytes 1572872 | tf_op jit(solution)/shard_map/ppermute | solution.py:349
  47.9 7.7 %collective-permute-start.2 = (bf16[8,256,128]{2,1,0:T(8,128)(2,1)S(1)}, bf16[8,256,128]{2,1,0:T(8,128)(2,1)S(1)}, u32[]{:S(2)}, u32[]{:S(2)}) collective-permute-start(bf16[8,256,128]{2,1,0:T(8,128)(2,1)S(1)} %collective-permute-done.1.arrived), channel_id=1, source_target_pairs={{1,0},{0,1},{3,2},{2,3},{5,4},{4,5},{7,6},{6,7},{9,8},{8,9},{11,10... | collective-permute-start | bytes 1572872 | tf_op jit(solution)/shard_map/ppermute | solution.py:349
  52.1 9.5 %all-to-all-start.2 = ((bf16[16,32,128]{2,1,0:T(8,128)(2,1)}), bf16[16,32,128]{2,1,0:T(8,128)(2,1)S(1)}, u32[]{:S(2)}, u32[]{:S(2)}) async-start(bf16[16,32,128]{2,1,0:T(8,128)(2,1)} %sum_copies.3), calls=%async_computation.2 | async-start | bytes 262144 | tf_op jit(solution)/shard_map/all_to_all | solution.py:380

commit v6 on v5

--- a/solution.py
+++ b/solution.py
@@ -193,14 +193,14 @@
     )(first, taps, edges, sources, jnp.asarray(turns), jnp.asarray(tap_turns), raw)
 
 
-def coherence_kernel(odd, offsets, edges, own, other, arrived, swapped, out, ext, high, low):
+def coherence_kernel(odd, offsets, edges, own, arrived, sibling, out, ext, high, low):
     for f in range(FRAMES):
         ext[0, f] = own[f]
-        ext[2, f] = swapped[f]
+        ext[2, f] = sibling[1, f]
 
     @pl.when(odd[0] == 0)
     def _():
-        ext[1] = other[...]
+        ext[1] = sibling[0]
 
     @pl.when(odd[0] == 1)
     def _():
@@ -255,11 +255,11 @@
         out[p, BANDS:, :] = total[:, WIDTH:] * scale
 
 
-def coherences(odd, offsets, edges, own, other, arrived, swapped):
+def coherences(odd, offsets, edges, own, arrived, sibling):
     return pl.pallas_call(
         coherence_kernel,
         out_shape=jax.ShapeDtypeStruct((OFFS, 2 * BANDS, WIDTH), F32),
-        in_specs=[SMEM] * 3 + [VMEM] * 4,
+        in_specs=[SMEM] * 3 + [VMEM] * 3,
         out_specs=VMEM,
         scratch_shapes=[
             pltpu.VMEM((3, FRAMES, NFFT, WIDTH), BF16),
@@ -268,7 +268,7 @@
         ],
         compiler_params=pltpu.CompilerParams(vmem_limit_bytes=VMEM_LIMIT),
         name="coherence",
-    )(odd, offsets, edges, own, other, arrived, swapped)
+    )(odd, offsets, edges, own, arrived, sibling)
 
 
 S_STEP = 8
@@ -385,11 +385,10 @@
     first = jnp.full((1,), lax.axis_index("ch") * WIDTH, jnp.int32)
     white, picked = whiten(raw, taps, edges, sources, first)
     odd = jnp.full((1,), lax.axis_index("ch") % 2, jnp.int32)
-    arrived = from_next_chip(white)
-    other = swap_in_chip(white)
-    held, found = spread_sources(picked, lambda: (other, arrived))
-    other, arrived = held
-    coherence = coherences(odd, offsets, edges, white, other, arrived, swap_in_chip(arrived))
+    landing = from_next_chip(white)
+    arrived, found = spread_sources(picked, lambda: landing)
+    sibling = swap_in_chip(jnp.stack([white, arrived]))
+    coherence = coherences(odd, offsets, edges, white, arrived, sibling)
     coherence, found = lax.optimization_barrier((coherence, found))
     correlation = correlations(found, white)
     return (coherence, correlation)

time: 65 us -> 65.2 us (level)
  starting transfers between devices: 32.7 us -> 29 us
  blocking collectives: 16.7 us -> 19 us
  other arithmetic: 0 us -> 1.18 us
    ppermute x2 -> x1, starting transfers between devices: 6.28 us -> 2.63 us  [swap_in_chip(): lax.ppermute(block, 'ch', [(i ^ 1, i) for i in range(lax.axis_size('ch'))])]
    all_to_all x1, blocking collectives: 16.7 us -> 19 us  [spread_sources(): lax.all_to_all(copies, 'ch', 0, 0, axis_index_groups=places, tiled=True)]
    another operation x0 -> x1, other arithmetic: none -> 1.18 us  [per_device(): sibling = swap_in_chip(jnp.stack([white, arrived]))]
  transfers between devices with their start and end apart: 5 -> 4, of which waited for: 1 -> 1; matrix products, arithmetic and copies ran while one was open for 0% -> 0% of each run, Pallas kernels for 10% -> 10%
where the time goes in v6:
time: 65.2 us; the launch traced here: 64.5 us
  starting transfers between devices  29 us (44%)
  blocking collectives  19 us (29%)
  Pallas kernels  14.4 us (22%)
  other arithmetic  1.18 us (2%)
  between operations  0.75 us (1%)
    all_to_all x1, blocking collectives, spread_sources(): lax.all_to_all(copies, 'ch', 0, 0, axis_index_groups=places, tiled=True)  19 us
    ppermute x1, starting transfers between devices, from_next_chip(): return lax.ppermute(block, 'ch', route)  12.7 us
    all_to_all x1, starting transfers between devices, spread_sources(): mine = lax.all_to_all(mine, 'ch', 0, 0, axis_index_groups=runs, tiled=True)  10.3 us
    pallas_call x1, Pallas kernels, coherences(): pl.pallas_call(coherence_kernel, out_shape=jax.ShapeDtypeStruct((OFFS, 2...  5.97 us
    pallas_call x1, Pallas kernels, whiten(): pl.pallas_call(whiten_kernel, out_shape=(jax.ShapeDtypeStruct((FRAMES, NF...  4.69 us
    all_to_all x1, starting transfers between devices, spread_sources(): lax.all_to_all(copies, 'ch', 0, 0, axis_index_groups=runs, tiled=True)  3.42 us
    pallas_call x1, Pallas kernels, correlations(): pl.pallas_call(correlate_kernel, out_shape=jax.ShapeDtypeStruct((LAGS, SO...  2.99 us
    ppermute x1, starting transfers between devices, swap_in_chip(): lax.ppermute(block, 'ch', [(i ^ 1, i) for i in range(lax.axis_size('ch'))])  2.63 us
  transfers between devices with their start and end apart: 4, of which 1 were waited for; matrix products, arithmetic and copies ran while one was open for 0% of the time, Pallas kernels for 10%

profile of v6, /device:TPU:1, one launch (start us, length us, event | category | flops | bytes accessed | tf_op | source)
XLA Modules:
  0.0 64.5 jit_solution(15018081270784407460)
XLA Ops:
  0.6 4.7 %whiten.1 = (bf16[8,256,128]{2,1,0:T(8,128)(2,1)}, bf16[16,32,128]{2,1,0:T(8,128)(2,1)}) custom-call(s32[1]{0:T(128)} %bitcast.1.first, f32[16]{0:T(128)} %taps_hbm.1, s32[17]{0:T(128)} %edges.1, s32[32]{0:T(128)} %sources_hbm.1, f32[2,128,640]{2,1,0:T(8,128)} %constant.25.clone.turns_hbm, f32[256,16]{1,0:T(8,128)} %constant.26.clone.tap_turns_hbm, ...), custom_call_target="tpu_custom_call" | custom-call | tf_op jit(solution)/shard_map/whiten/pallas_call | solution.py:173
  5.3 0.0 copy-start
  5.3 0.0 copy-start.2
  5.4 0.0 copy-start.3
  5.4 10.3 %all-to-all-start = ((bf16[16,32,128]{2,1,0:T(8,128)(2,1)}), bf16[16,32,128]{2,1,0:T(8,128)(2,1)S(1)}, u32[]{:S(2)}, u32[]{:S(2)}) async-start(bf16[16,32,128]{2,1,0:T(8,128)(2,1)} %get-tuple-element.9), calls=%async_computation | async-start | bytes 262144 | tf_op jit(solution)/shard_map/all_to_all | solution.py:375
  15.7 12.7 %collective-permute-start = (bf16[8,256,128]{2,1,0:T(8,128)(2,1)}, bf16[8,256,128]{2,1,0:T(8,128)(2,1)S(1)}, u32[]{:S(2)}, u32[]{:S(2)}) collective-permute-start(bf16[8,256,128]{2,1,0:T(8,128)(2,1)} %get-tuple-element.8.own.white), channel_id=1, source_target_pairs={{3,0},{2,1},{5,2},{4,3},{7,4},{6,5},{9,6},{8,7},{11,8},{10,9},{13,... | collective-permute-start | bytes 1572872 | tf_op jit(solution)/shard_map/ppermute | solution.py:345
  28.4 0.0 all-to-all-done.parts
  28.4 19.0 %all_to_all.15.parts = bf16[32,32,128]{2,1,0:T(8,128)(2,1)S(1)} all-to-all(bf16[32,32,128]{2,1,0:T(8,128)(2,1)S(1)} %sum_copies.2), channel_id=1, replica_groups={{0,16,32,48,64,80,96,112,128,144,160,176,192,208,224,240,256,272,288,30..., dimensions={0} | all-to-all | bytes 524288 | tf_op jit(solution)/shard_map/all_to_all | solution.py:377
  47.4 0.7 %sum_copies.3 = bf16[16,32,128]{2,1,0:T(8,128)(2,1)} custom-call(bf16[32,32,128]{2,1,0:T(8,128)(2,1)S(1)} %all_to_all.15.parts), custom_call_target="tpu_custom_call" | custom-call | flops 10000 | bytes 1048576 | tf_op jit(solution)/shard_map/sum_copies/pallas_call | solution.py:358
  48.1 0.0 collective-permute-done.arrived
  48.1 0.0 copy-start.1
  48.1 1.2 %pad_maximum_fusion = bf16[2,8,256,128]{3,2,1,0:T(8,128)(2,1)S(1)} fusion(bf16[1,8,256,128]{3,2,1,0:T(8,128)(2,1)S(1)} %bitcast.6, bf16[1,8,256,128]{3,2,1,0:T(8,128)(2,1)} %bitcast.5), kind=kLoop, calls=%fused_computation | loop fusion | flops 524288 | bytes 2097152 | tf_op jit(solution)/shard_map/stack | solution.py:390
  49.3 2.6 %collective-permute-start.1 = (bf16[2,8,256,128]{3,2,1,0:T(8,128)(2,1)S(1)}, bf16[2,8,256,128]{3,2,1,0:T(8,128)(2,1)S(1)}, u32[]{:S(2)}, u32[]{:S(2)}) collective-permute-start(bf16[2,8,256,128]{3,2,1,0:T(8,128)(2,1)S(1)} %pad_maximum_fusion), channel_id=1, source_target_pairs={{1,0},{0,1},{3,2},{2,3},{5,4},{4,5},{7,6},{6,7},{9,8},{8,9},{11,10... | collective-permute-start | bytes 3145736 | tf_op jit(solution)/shard_map/ppermute | solution.py:349
  52.0 3.4 %all-to-all-start.2 = ((bf16[16,32,128]{2,1,0:T(8,128)(2,1)}), bf16[16,32,128]{2,1,0:T(8,128)(2,1)S(1)}, u32[]{:S(2)}, u32[]{:S(2)}) async-start(bf16[16,32,128]{2,1,0:T(8,128)(2,1)} %sum_copies.3), calls=%async_computation.2 | async-start | bytes 262144 | tf_op jit(solution)/shard_map/all_to_all | solution.py:380
  55.4 0.0 collective-permute-done.1.sibling
  55.4 0.0 copy-done
  55.4 0.0 copy-done.2
  55.4 0.0 copy-done.3
  55.4 6.0 %coherence.1 = f32[16,32,128]{2,1,0:T(8,128)} custom-call(s32[1]{0:T(128)} %bitcast.odd, s32[16]{0:T(128)S(1)} %copy-done.3, s32[17]{0:T(128)S(1)} %copy-done.2, bf16[8,256,128]{2,1,0:T(8,128)(2,1)S(1)} %copy-done, bf16[8,256,128]{2,1,0:T(8,128)(2,1)S(1)} %collective-permute-done.arrived, bf16[2,8,256,128]{3,2,1,0:T(8,128)(2,1)S(1)} %collective-permute-done.1.sibling), custom_call_target="tpu_custom_call" | custom-call | tf_op jit(solution)/shard_map/coherence/pallas_call | solution.py:259
  61.4 0.1 all-to-all-done.2.sources
  61.5 0.0 copy-done.1
  61.5 3.0 %correlate.1 = f32[129,32,128]{2,1,0:T(8,128)} custom-call(bf16[288,256]{1,0:T(8,128)(2,1)S(1)} %copy-done.1, bf16[16,32,128]{2,1,0:T(8,128)(2,1)S(1)} %all-to-all-done.2.sources, bf16[8,256,128]{2,1,0:T(8,128)(2,1)S(1)} %copy-done), custom_call_target="tpu_custom_call" | custom-call | tf_op jit(solution)/shard_map/correlate/pallas_call | solution.py:325
  (1 shorter events, 0.0 us)
Async XLA Ops:
  5.3 50.1 %copy-start = (bf16[8,256,128]{2,1,0:T(8,128)(2,1)S(1)}, bf16[8,256,128]{2,1,0:T(8,128)(2,1)}, u32[]{:S(2)}) copy-start(bf16[8,256,128]{2,1,0:T(8,128)(2,1)} %get-tuple-element.8.own.white) | copy-start | bytes 1572868
  5.3 50.1 %copy-start.2 = (s32[17]{0:T(128)S(1)}, s32[17]{0:T(128)}, u32[]{:S(2)}) copy-start(s32[17]{0:T(128)} %edges.1) | copy-start | bytes 208
  5.4 50.1 %copy-start.3 = (s32[16]{0:T(128)S(1)}, s32[16]{0:T(128)}, u32[]{:S(2)}) copy-start(s32[16]{0:T(128)} %offsets.1) | copy-start | bytes 196
  5.4 23.0 %all-to-all-start = ((bf16[16,32,128]{2,1,0:T(8,128)(2,1)}), bf16[16,32,128]{2,1,0:T(8,128)(2,1)S(1)}, u32[]{:S(2)}, u32[]{:S(2)}) async-start(bf16[16,32,128]{2,1,0:T(8,128)(2,1)} %get-tuple-element.9), calls=%async_computation | async-start | bytes 262144 | tf_op jit(solution)/shard_map/all_to_all | solution.py:375
  15.7 32.4 %collective-permute-start = (bf16[8,256,128]{2,1,0:T(8,128)(2,1)}, bf16[8,256,128]{2,1,0:T(8,128)(2,1)S(1)}, u32[]{:S(2)}, u32[]{:S(2)}) collective-permute-start(bf16[8,256,128]{2,1,0:T(8,128)(2,1)} %get-tuple-element.8.own.white), channel_id=1, source_target_pairs={{3,0},{2,1},{5,2},{4,3},{7,4},{6,5},{9,6},{8,7},{11,8},{10,9},{13,... | collective-permute-start | bytes 1572872 | tf_op jit(solution)/shard_map/ppermute | solution.py:345
  48.1 13.4 %copy-start.1 = (bf16[288,256]{1,0:T(8,128)(2,1)S(1)}, bf16[288,256]{1,0:T(8,128)(2,1)}, u32[]{:S(2)}) copy-start(bf16[288,256]{1,0:T(8,128)(2,1)} %constant.27.clone.table) | copy-start | bytes 442372
  49.3 6.1 %collective-permute-start.1 = (bf16[2,8,256,128]{3,2,1,0:T(8,128)(2,1)S(1)}, bf16[2,8,256,128]{3,2,1,0:T(8,128)(2,1)S(1)}, u32[]{:S(2)}, u32[]{:S(2)}) collective-permute-start(bf16[2,8,256,128]{3,2,1,0:T(8,128)(2,1)S(1)} %pad_maximum_fusion), channel_id=1, source_target_pairs={{1,0},{0,1},{3,2},{2,3},{5,4},{4,5},{7,6},{6,7},{9,8},{8,9},{11,10... | collective-permute-start | bytes 3145736 | tf_op jit(solution)/shard_map/ppermute | solution.py:349
  52.0 9.5 %all-to-all-start.2 = ((bf16[16,32,128]{2,1,0:T(8,128)(2,1)}), bf16[16,32,128]{2,1,0:T(8,128)(2,1)S(1)}, u32[]{:S(2)}, u32[]{:S(2)}) async-start(bf16[16,32,128]{2,1,0:T(8,128)(2,1)} %sum_copies.3), calls=%async_computation.2 | async-start | bytes 262144 | tf_op jit(solution)/shard_map/all_to_all | solution.py:380
